TPU v7x, 256 devices: a whole 4x4x8 slice. The times are simulated.
256 devices in a mesh: graph: 32 (over z, y), attn: 8 (over x, core).
Axes of the slice: x: 4, y: 4, z: 8, core: 2. Of those that a mesh axis runs over, the one named last changes fastest.
Arguments:
- features: bfloat16 [131072, 1024], P(('graph', 'attn')), may hold values from -6 to 6
- send_rows: int32 [256, 32, 64], P(('graph', 'attn')), may hold values from 0 to 511
- send_count: int32 [256, 32], P(('graph', 'attn')), may hold values from 32 to 64, as said below
- edge_blocks: int32 [1024, 6], P(('graph', 'attn')), may hold values from 0 to 19, as said below
- edge_weight: int32 [1024, 6, 128, 128], P(('graph', 'attn')), may hold values from 0 to 3
- mask_blocks: int32 [32, 32, 16], P('graph'), may hold values from 0 to 31, as said below
- norm_gain: float32 [1024], replicated, may hold values from 0.5 to 1.5
- query_weight: bfloat16 [1024, 1024], replicated, may hold values from -1 to 1
- key_weight: bfloat16 [1024, 1024], replicated, may hold values from -3 to 3
- value_weight: bfloat16 [1024, 1024], replicated, may hold values from -0.1875 to 0.1875
- out_weight: bfloat16 [1024, 1024], replicated, may hold values from -0.1875 to 0.1875
Outputs:
- updated: bfloat16 [131072, 1024], P(('graph', 'attn'))
Inputs may be any that keep to these rules, and one draw needn't show every extreme that they name: `send_count`: each device sends at least half of its 64 slots, rounded up, to every partition; at least one partition gets all 64 slots from each device. `edge_blocks`: the 6 numbers of a destination block are distinct and the first is the destination block's own block; numbers below 4 name the device's own blocks, the others its halo blocks in order; every halo block of a device is named by some destination block of that device. `mask_blocks`: the 16 numbers of a query block are distinct and include the query block itself.
All inputs are finite; a program needn't handle non-finite values.
Results may differ from a plain program's by a relative error of at most 0.007.
Values may be sent and summed in bfloat16 or wider, within the bound.
A program may use at most 128 MiB of HBM per device.

v0:
```python
import jax
import jax.numpy as jnp
from jax import lax
from jax.sharding import PartitionSpec as P

HEAD_DIM = 64
BLOCK = 128


EPSILON = 1e-06


def gather_halo(features, row_lists, live_counts):
    groups = row_lists.shape[0]
    slot_count = row_lists.shape[1]
    picked = jnp.take(features, row_lists.reshape(-1), axis=0).reshape(
        groups, slot_count, features.shape[1]
    )
    living = jnp.arange(slot_count, dtype=jnp.int32)[None, :] < live_counts[:, None]
    return jnp.where(living[:, :, None], picked, jnp.zeros_like(picked))


def finish(features, summed, edge_weight):
    row_count, model_width = features.shape
    degree = jnp.sum(edge_weight, axis=(1, 3)).astype(jnp.float32)
    own_rows = features.reshape(-1, BLOCK, model_width).astype(jnp.float32)
    result = (own_rows + summed) * lax.rsqrt(1.0 + degree)[:, :, None]
    return result.reshape(row_count, model_width).astype(jnp.bfloat16)


def aggregate(features, halo, edge_blocks, edge_weight):
    model_width = features.shape[1]
    source = jnp.concatenate([features, halo], axis=0).reshape(-1, BLOCK, model_width)
    picked = jnp.take(source, edge_blocks.reshape(-1), axis=0).reshape(
        edge_blocks.shape + (BLOCK, model_width)
    )
    weights = edge_weight.astype(jnp.bfloat16)
    summed = jnp.einsum("bnij,bnjd->bid", weights, picked, preferred_element_type=jnp.float32)
    return finish(features, summed, edge_weight)


def normalize(aggregated, norm_gain):
    values = aggregated.astype(jnp.float32)
    scaled = values * lax.rsqrt(jnp.mean(values * values, axis=1, keepdims=True) + EPSILON)
    return (scaled * norm_gain).astype(jnp.bfloat16)


def attend_blocks(query_rows, key_rows, value_rows, mask):
    shard_rows, head_cols = query_rows.shape
    heads_here = head_cols // HEAD_DIM
    blocks = shard_rows // BLOCK
    group_size = 4
    key_blocks = key_rows.reshape(blocks, BLOCK, head_cols)
    value_blocks = value_rows.reshape(blocks, BLOCK, head_cols)
    score_scale = HEAD_DIM ** (-0.5)
    column_head = jnp.arange(head_cols, dtype=jnp.int32) // HEAD_DIM

    def one_group(group_index):
        first_block = group_index * group_size
        queries = lax.dynamic_slice_in_dim(query_rows, first_block * BLOCK, group_size * BLOCK, 0)
        queries = queries.reshape(group_size, BLOCK, head_cols)
        chosen = lax.dynamic_slice_in_dim(mask, first_block, group_size, 0).reshape(-1)
        keyset = jnp.take(key_blocks, chosen, axis=0).reshape(group_size, -1, head_cols)
        valueset = jnp.take(value_blocks, chosen, axis=0).reshape(group_size, -1, head_cols)
        mixed = jnp.zeros((group_size, BLOCK, head_cols), jnp.float32)
        for head in range(heads_here):
            selected = (column_head == head)[None, None, :]
            masked = jnp.where(selected, queries, jnp.zeros_like(queries))
            scores = (
                jnp.einsum("sqc,skc->sqk", masked, keyset, preferred_element_type=jnp.float32)
                * score_scale
            )
            row_max = jnp.max(scores, axis=-1, keepdims=True)
            raised = jnp.exp(scores - row_max)
            probs = (raised / jnp.sum(raised, axis=-1, keepdims=True)).astype(jnp.bfloat16)
            product = jnp.einsum(
                "sqk,skc->sqc", probs, valueset, preferred_element_type=jnp.float32
            )
            mixed = mixed + jnp.where(selected, product, 0.0)
        return mixed.astype(jnp.bfloat16).reshape(group_size * BLOCK, head_cols)

    results = lax.map(one_group, jnp.arange(blocks // group_size, dtype=jnp.int32))
    return results.reshape(shard_rows, head_cols)


def on_device(
    features,
    send_rows,
    send_count,
    edge_blocks,
    edge_weight,
    mask_blocks,
    norm_gain,
    query_weight,
    key_weight,
    value_weight,
    out_weight,
):
    outgoing = gather_halo(features, send_rows[0], send_count[0])
    model_width = features.shape[1]
    incoming = lax.all_to_all(outgoing, "graph", split_axis=0, concat_axis=0, tiled=True)
    halo = incoming.reshape(-1, model_width)
    aggregated = aggregate(features, halo, edge_blocks, edge_weight)
    normed = normalize(aggregated, norm_gain)
    head_width = query_weight.shape[1] // lax.axis_size("attn")
    first_col = lax.axis_index("attn") * head_width
    own_columns = jnp.concatenate(
        [
            lax.dynamic_slice_in_dim(matrix, first_col, head_width, 1)
            for matrix in (query_weight, key_weight, value_weight)
        ],
        axis=1,
    )
    joined = jnp.dot(
        lax.all_gather(normed, "attn", axis=0, tiled=True),
        own_columns,
        preferred_element_type=jnp.float32,
    ).astype(jnp.bfloat16)
    query_rows = joined[:, :head_width]
    key_rows = joined[:, head_width : 2 * head_width]
    value_rows = joined[:, 2 * head_width :]
    attended = attend_blocks(query_rows, key_rows, value_rows, mask_blocks[0])
    returned = lax.all_to_all(attended, "attn", split_axis=0, concat_axis=1, tiled=True)
    updated = jnp.dot(returned, out_weight, preferred_element_type=jnp.float32) + aggregated.astype(
        jnp.float32
    )
    return updated.astype(jnp.bfloat16)


def solution(mesh):
    placed = (
        P(("graph", "attn"), None),
        P(("graph", "attn"), None, None),
        P(("graph", "attn"), None),
        P(("graph", "attn"), None),
        P(("graph", "attn"), None, None, None),
        P("graph", None, None),
        P(),
        P(),
        P(),
        P(),
        P(),
    )
    return jax.shard_map(
        on_device, mesh=mesh, in_specs=placed, out_specs=P(("graph", "attn"), None), check_vma=False
    )
```

profile of v0, /device:TPU:1, one launch (start us, length us, event | category | flops | bytes accessed | tf_op | source)
XLA Modules:
  0.0 490.6 jit_solution(1515339954339208438)
XLA Ops:
  8.3 12.3 %gather_fusion.2 = bf16[2048,1024]{1,0:T(8,128)(2,1)} fusion(bf16[512,1024]{1,0:T(8,128)(2,1)} %param.15, s32[2048]{0:T(1024)S(1)} %broadcast_clamp_fusion), kind=kCustom, calls=%fused_computation.2 | custom fusion | bytes 8396800 | tf_op jit(solution)/shard_map/jit(_take)/gather | solution.py:16
  20.6 3.9 select_select_fusion
  24.6 12.3 %all-to-all-start = ((bf16[32,64,1024]{2,1,0:T(8,128)(2,1)}), bf16[32,64,1024]{2,1,0:T(8,128)(2,1)}, u32[]{:S(2)}, u32[]{:S(2)}) async-start(bf16[32,64,1024]{2,1,0:T(8,128)(2,1)} %select_select_fusion), calls=%async_computation | async-start | bytes 8388608 | tf_op jit(solution)/shard_map/all_to_all | solution.py:101
  38.7 91.2 %all-to-all-done = bf16[32,64,1024]{2,1,0:T(8,128)(2,1)} async-done(((bf16[32,64,1024]{2,1,0:T(8,128)(2,1)}), bf16[32,64,1024]{2,1,0:T(8,128)(2,1)}, u32[]{:S(2)}, u32[]{:S(2)}) %all-to-all-start) | async-done | bytes 4194336 | tf_op jit(solution)/shard_map/all_to_all | solution.py:101
  129.9 5.2 %pad_maximum_fusion = bf16[2560,1024]{1,0:T(8,128)(2,1)} fusion(bf16[2048,1024]{1,0:T(8,128)(2,1)} %bitcast.5, bf16[512,1024]{1,0:T(8,128)(2,1)S(1)} %copy-done.1), kind=kLoop, calls=%fused_computation.57 | loop fusion | flops 10485760 | bytes 10485760 | tf_op jit(solution)/shard_map/concatenate | solution.py:33
  135.1 6.9 %gather_fusion.3 = bf16[24,128,1024]{2,1,0:T(8,128)(2,1)} fusion(bf16[20,128,1024]{2,1,0:T(8,128)(2,1)} %bitcast.82, s32[1024]{0:T(1024)S(1)} %pad_clamp_fusion.1), kind=kCustom, calls=%fused_computation.3 | custom fusion | bytes 12583008 | tf_op jit(solution)/shard_map/jit(_take)/gather | solution.py:34
  142.0 5.1 %fusion.40 = (f32[4,128]{1,0:T(4,128)S(1)}, bf16[4,128,1024]{2,1,0:T(8,128)(2,1)S(1)}) fusion(f32[4,128]{1,0:T(4,128)S(1)} %add_rsqrt_fusion, bf16[4,6,128,1024]{3,2,1,0:T(8,128)(2,1)} %bitcast.84, pred[4,6]{1,0:T(4,128)(4,1)S(1)} %compare_and_fusion.2, s32[4,6,128,128]{3,2,1,0:T(8,128)} %param.19, bf16[4,128,1024]{2,1,0:T(8,128)(2,1)S(1)} %bitcast.73), kind=kOutput, calls=%fused_computation.66 | convolution fusion | flops 812514816 | bytes 9965592 | tf_op jit(solution)/shard_map/bnij,bnjd->bid/dot_general | solution.py:38
  151.7 50.5 %all-gather.2.cloned.1.call-done = bf16[4096,1024]{1,0:T(8,128)(2,1)} async-done(((bf16[512,1024]{1,0:T(8,128)(2,1)}), bf16[4096,1024]{1,0:T(8,128)(2,1)}) %all-gather.2.cloned.1.call-update) | async-done | bytes 8388624 | tf_op jit(solution)/shard_map/all_gather | solution.py:115
  202.1 8.3 %convolution_convert_fusion = bf16[4096,384]{1,0:T(8,128)(2,1)S(1)} fusion(bf16[4096,1024]{1,0:T(8,128)(2,1)} %all-gather.2.cloned.1.call-done, bf16[1024,128]{1,0:T(8,128)(2,1)S(1)} %get-tuple-element.184, bf16[1024,128]{1,0:T(8,128)(2,1)S(1)} %get-tuple-element.185, bf16[1024,128]{1,0:T(8,128)(2,1)S(1)} %constant_dynamic-slice_fusion.4), kind=kOutput, calls=%fused_computation.56 | convolution fusion | flops 3225157632 | bytes 12320768 | tf_op jit(solution)/shard_map/dot_general | solution.py:114
  212.3 250.3 %while.14 = (s32[]{:T(128)}, bf16[8,512,128]{1,2,0:T(8,128)(2,1)}, s32[8]{0:T(128)S(1)}, bf16[4096,128]{1,0:T(8,128)(2,1)}, s32[32,16]{1,0:T(8,128)S(1)}, /*inde...) while((s32[]{:T(128)}, bf16[8,512,128]{1,2,0:T(8,128)(2,1)}, ...), condition=%wide.region_7.9_spmd.clone.clone, body=%wide.region_2.0_spmd.clone.clone.sunk | while | flops 1086724864 | bytes 43663468 | solution.py:82
  219.2 4.6 broadcast_select_fusion.23
  225.4 4.8 fusion.77
  230.1 4.3 fusion.78
  234.5 4.8 fusion.79
  239.2 3.6 fusion.80
  250.5 4.6 broadcast_select_fusion.23
  256.6 4.8 fusion.77
  261.4 4.3 fusion.78
  265.7 4.8 fusion.79
  270.5 3.6 fusion.80
  281.8 4.6 broadcast_select_fusion.23
  287.9 4.8 fusion.77
  292.7 4.3 fusion.78
  297.0 4.8 fusion.79
  301.8 3.6 fusion.80
  313.0 4.6 broadcast_select_fusion.23
  319.2 4.8 fusion.77
  324.0 4.3 fusion.78
  328.3 4.8 fusion.79
  333.1 3.6 fusion.80
  344.3 4.6 broadcast_select_fusion.23
  350.5 4.8 fusion.77
  355.3 4.3 fusion.78
  359.6 4.8 fusion.79
  364.4 3.6 fusion.80
  375.6 4.6 broadcast_select_fusion.23
  381.8 4.8 fusion.77
  386.6 4.3 fusion.78
  390.9 4.8 fusion.79
  406.9 4.6 broadcast_select_fusion.23
  413.1 4.8 fusion.77
  417.8 4.3 fusion.78
  422.2 4.8 fusion.79
  438.2 4.6 broadcast_select_fusion.23
  444.3 4.8 fusion.77
  449.1 4.3 fusion.78
  453.4 4.8 fusion.79
  462.6 18.9 %all_to_all.21 = bf16[8,512,128]{1,2,0:T(8,128)(2,1)S(1)} all-to-all(bf16[8,512,128]{1,2,0:T(8,128)(2,1)} %get-tuple-element.116), channel_id=1, replica_groups=mesh['graph'=32,'attn'=8] {'attn'}, dimensions={0} | all-to-all | bytes 2097152 | tf_op jit(solution)/shard_map/all_to_all | solution.py:123
  (134 shorter events, 86.4 us)
Async XLA Ops:
  6.5 474.9 %copy-start = (bf16[1024,1024]{1,0:T(8,128)(2,1)S(1)}, bf16[1024,1024]{1,0:T(8,128)(2,1)}, u32[]{:S(2)}) copy-start(bf16[1024,1024]{1,0:T(8,128)(2,1)} %param.25) | copy-start | bytes 6291460
  24.6 12.4 %copy-start.5 = (s32[4,6]{1,0:T(4,128)S(1)}, s32[4,6]{1,0:T(4,128)}, u32[]{:S(2)}) copy-start(s32[4,6]{1,0:T(4,128)} %param.18) | copy-start | bytes 292
  24.6 105.3 %all-to-all-start = ((bf16[32,64,1024]{2,1,0:T(8,128)(2,1)}), bf16[32,64,1024]{2,1,0:T(8,128)(2,1)}, u32[]{:S(2)}, u32[]{:S(2)}) async-start(bf16[32,64,1024]{2,1,0:T(8,128)(2,1)} %select_select_fusion), calls=%async_computation | async-start | bytes 8388608 | tf_op jit(solution)/shard_map/all_to_all | solution.py:101
  36.9 93.0 %copy-start.1 = (bf16[512,1024]{1,0:T(8,128)(2,1)S(1)}, bf16[512,1024]{1,0:T(8,128)(2,1)}, u32[]{:S(2)}) copy-start(bf16[512,1024]{1,0:T(8,128)(2,1)} %param.15) | copy-start | bytes 3145732
  36.9 165.3 %all-gather.2.cloned.1.call-start = ((), (), s32[]{:S(2)}) async-start(), calls=%async_computation.2 | async-start | bytes 9437184 | tf_op jit(solution)/shard_map/all_gather | solution.py:115
  142.0 6.1 %copy-start.6 = (f32[1024]{0:T(1024)S(1)}, f32[1024]{0:T(1024)}, u32[]{:S(2)}) copy-start(f32[1024]{0:T(1024)} %param.21) | copy-start | bytes 12292
  147.1 1.0 copy-start.2
  147.1 2.4 copy-start.4
  462.6 18.9 %copy-start.3 = (bf16[4,128,1024]{2,1,0:T(8,128)(2,1)S(1)}, bf16[4,128,1024]{2,1,0:T(8,128)(2,1)}, u32[]{:S(2)}) copy-start(bf16[4,128,1024]{2,1,0:T(8,128)(2,1)} %copy-done.2) | copy-start | bytes 3145732
Sparse Core Ops, SparseCore 0:
  149.6 52.4 all-gather.1
where the time goes:
time: 492 us; the launch traced here: 491 us
  matrix products  155 us (32%)
  waiting for transfers between devices  142 us (29%)
  local copies, waits for them, and re-layouts  88.5 us (18%)
  other arithmetic  50.2 us (10%)
  blocking collectives  18.9 us (4%)
  between operations  13.5 us (3%)
  starting transfers between devices  12.3 us (2%)
  loops' own time  10.2 us (2%)
    all_to_all x1, waiting for transfers between devices, on_device(): lax.all_to_all(outgoing, 'graph', split_axis=0, concat_axis=0, tiled=True)  91.2 us
    sub x16, matrix products, one_group(): raised = jnp.exp(scores - row_max)  76.3 us
    dot_general x16, matrix products, one_group(): jnp.einsum('sqk,skc->sqc', probs, valueset, preferred_element_type=jnp.fl...  63.3 us
    all_gather x1, waiting for transfers between devices, on_device(): lax.all_gather(normed, 'attn', axis=0, tiled=True)  50.5 us
    select_n x16, other arithmetic, one_group(): jnp.take(key_blocks, chosen, axis=0).reshape(group_size, -1, head_cols)  37.1 us
    gather x8, local copies, waits for them, and re-layouts, one_group(): jnp.take(key_blocks, chosen, axis=0).reshape(group_size, -1, head_cols)  27.1 us
    all_to_all x1, blocking collectives, on_device(): lax.all_to_all(attended, 'attn', split_axis=0, concat_axis=1, tiled=True)  18.9 us
    gather x8, local copies, waits for them, and re-layouts, one_group(): jnp.take(value_blocks, chosen, axis=0).reshape(group_size, -1, head_cols)  17 us
  transfers between devices with their start and end apart: 2, of which 2 were waited for; matrix products, arithmetic and copies ran while one was open for 1% of the time, Pallas kernels for 0%

commit v1 on v0

v1 whole, which is shorter than its diff:
```python
import jax
import jax.numpy as jnp
from jax import lax
from jax.experimental import pallas as pl
from jax.experimental.pallas import tpu as pltpu
from jax.sharding import PartitionSpec as P

HEAD_DIM = 64
BLOCK = 128


EPSILON = 1e-06


def gather_halo(features, row_lists, live_counts):
    groups, slot_count = row_lists.shape
    row_count = features.shape[0]
    living = jnp.arange(slot_count, dtype=jnp.int32)[None, :] < live_counts[:, None]
    chosen = jnp.where(living, row_lists, -1).reshape(-1)
    pick = (chosen[:, None] == jnp.arange(row_count, dtype=jnp.int32)[None, :]).astype(jnp.bfloat16)
    picked = jnp.dot(pick, features, preferred_element_type=jnp.float32).astype(jnp.bfloat16)
    return picked.reshape(groups, slot_count, features.shape[1])


def finish(features, summed, edge_weight):
    row_count, model_width = features.shape
    degree = jnp.sum(edge_weight, axis=(1, 3)).astype(jnp.float32)
    own_rows = features.reshape(-1, BLOCK, model_width).astype(jnp.float32)
    result = (own_rows + summed) * lax.rsqrt(1.0 + degree)[:, :, None]
    return result.reshape(row_count, model_width).astype(jnp.bfloat16)


def aggregate(features, halo, edge_blocks, edge_weight):
    model_width = features.shape[1]
    source = jnp.concatenate([features, halo], axis=0).reshape(-1, BLOCK, model_width)
    picked = jnp.take(source, edge_blocks.reshape(-1), axis=0).reshape(
        edge_blocks.shape + (BLOCK, model_width)
    )
    weights = edge_weight.astype(jnp.bfloat16)
    summed = jnp.einsum("bnij,bnjd->bid", weights, picked, preferred_element_type=jnp.float32)
    return finish(features, summed, edge_weight)


def normalize(aggregated, norm_gain):
    values = aggregated.astype(jnp.float32)
    scaled = values * lax.rsqrt(jnp.mean(values * values, axis=1, keepdims=True) + EPSILON)
    return (scaled * norm_gain).astype(jnp.bfloat16)


def attend_kernel(mask_ref, joined_ref, out_ref, scores_a, scores_b):
    width = 2 * HEAD_DIM
    blocks, keys = mask_ref.shape
    first = lax.broadcasted_iota(jnp.int32, (BLOCK, width), 1) < HEAD_DIM
    ones = jnp.ones((2 * BLOCK, width), jnp.bfloat16)

    def rows_of(block):
        return pl.ds(pl.multiple_of(block * BLOCK, BLOCK), BLOCK)

    def pair(block, step, column):
        cols = slice(column * width, (column + 1) * width)
        low = joined_ref[rows_of(mask_ref[block, 2 * step]), cols]
        high = joined_ref[rows_of(mask_ref[block, 2 * step + 1]), cols]
        return jnp.concatenate([low, high], axis=0)

    def score(block, scores):
        query = joined_ref[rows_of(block), 0:width] * jnp.bfloat16(HEAD_DIM ** (-0.5))
        zero = jnp.zeros_like(query)
        query = jnp.concatenate(
            [jnp.where(first, query, zero), jnp.where(first, zero, query)], axis=0
        )
        top = None
        for step in range(keys // 2):
            part = lax.dot_general(
                query, pair(block, step, 1), (((1,), (1,)), ((), ())),
                preferred_element_type=jnp.float32,
            )
            scores[:, 2 * step * BLOCK : (2 * step + 2) * BLOCK] = part
            part = jnp.maximum(part[:, :BLOCK], part[:, BLOCK:])
            top = part if top is None else jnp.maximum(top, part)
        return jnp.max(top, axis=1, keepdims=True)

    def mix(block, scores, top):
        total = jnp.zeros((2 * BLOCK, 2 * width), jnp.float32)
        for step in range(keys // 2):
            values = jnp.concatenate([pair(block, step, 2), ones], axis=1)
            part = scores[:, 2 * step * BLOCK : (2 * step + 2) * BLOCK]
            raised = jnp.exp(part - top).astype(jnp.bfloat16)
            total = total + jnp.dot(raised, values, preferred_element_type=jnp.float32)
        result = total[:, :width] / total[:, width:]
        out_ref[rows_of(block), :] = jnp.where(first, result[:BLOCK], result[BLOCK:]).astype(
            jnp.bfloat16
        )

    def two(index, carry):
        top_a = score(2 * index, scores_a)
        top_b = score(2 * index + 1, scores_b)
        mix(2 * index, scores_a, top_a)
        mix(2 * index + 1, scores_b, top_b)
        return carry

    lax.fori_loop(0, blocks // 2, two, 0)


def attend_blocks(joined, mask):
    keys = mask.shape[1] * BLOCK
    return pl.pallas_call(
        attend_kernel,
        out_shape=jax.ShapeDtypeStruct((joined.shape[0], 2 * HEAD_DIM), jnp.bfloat16),
        in_specs=[
            pl.BlockSpec(memory_space=pltpu.SMEM),
            pl.BlockSpec(memory_space=pltpu.VMEM),
        ],
        out_specs=pl.BlockSpec(memory_space=pltpu.VMEM),
        scratch_shapes=[pltpu.VMEM((2 * BLOCK, keys), jnp.float32)] * 2,
        compiler_params=pltpu.CompilerParams(vmem_limit_bytes=40 * 2**20),
    )(mask, joined)


def on_device(
    features,
    send_rows,
    send_count,
    edge_blocks,
    edge_weight,
    mask_blocks,
    norm_gain,
    query_weight,
    key_weight,
    value_weight,
    out_weight,
):
    outgoing = gather_halo(features, send_rows[0], send_count[0])
    model_width = features.shape[1]
    incoming = lax.all_to_all(outgoing, "graph", split_axis=0, concat_axis=0, tiled=True)
    halo = incoming.reshape(-1, model_width)
    aggregated = aggregate(features, halo, edge_blocks, edge_weight)
    normed = normalize(aggregated, norm_gain)
    head_width = query_weight.shape[1] // lax.axis_size("attn")
    first_col = lax.axis_index("attn") * head_width
    own_columns = jnp.concatenate(
        [
            lax.dynamic_slice_in_dim(matrix, first_col, head_width, 1)
            for matrix in (query_weight, key_weight, value_weight)
        ],
        axis=1,
    )
    joined = jnp.dot(
        lax.all_gather(normed, "attn", axis=0, tiled=True),
        own_columns,
        preferred_element_type=jnp.float32,
    ).astype(jnp.bfloat16)
    attended = attend_blocks(joined, mask_blocks[0])
    returned = lax.all_to_all(attended, "attn", split_axis=0, concat_axis=1, tiled=True)
    updated = jnp.dot(returned, out_weight, preferred_element_type=jnp.float32) + aggregated.astype(
        jnp.float32
    )
    return updated.astype(jnp.bfloat16)


def solution(mesh):
    placed = (
        P(("graph", "attn"), None),
        P(("graph", "attn"), None, None),
        P(("graph", "attn"), None),
        P(("graph", "attn"), None),
        P(("graph", "attn"), None, None, None),
        P("graph", None, None),
        P(),
        P(),
        P(),
        P(),
        P(),
    )
    return jax.shard_map(
        on_device, mesh=mesh, in_specs=placed, out_specs=P(("graph", "attn"), None), check_vma=False
    )
```

time: 492 us -> 253 us (0.51)
  matrix products: 155 us -> 20.9 us
  local copies, waits for them, and re-layouts: 88.5 us -> 12.5 us
  other arithmetic: 50.2 us -> 8.93 us
  Pallas kernels: 0 us -> 23.7 us
  loops' own time: 10.2 us -> 0 us
    sub x16 -> x0, matrix products: 76.3 us -> none  [one_group(): raised = jnp.exp(scores - row_max)]
    dot_general x16 -> x1, matrix products: 63.3 us -> 5.2 us  [gather_halo(): jnp.dot(pick, features, preferred_element_type=jnp.float32)]
    gather x17 -> x0, local copies, waits for them, and re-layouts: 56.4 us -> none  [the longest x8 27.1 us: one_group(): jnp.take(key_blocks, chosen, axis=0).reshape(group_size, -1, head_cols)]
    select_n x18 -> x1, other arithmetic: 41 us -> 0.01 us  [gather_halo(): chosen = jnp.where(living, row_lists, -1).reshape(-1)]
    pallas_call x0 -> x1, Pallas kernels: none -> 23.7 us  [attend_blocks(): pl.pallas_call(attend_kernel, out_shape=jax.ShapeDtypeStruct((joined.shap...]
    dynamic_slice x24 -> x0, local copies, waits for them, and re-layouts: 12.3 us -> none  [the longest x8 7.35 us: one_group(): lax.dynamic_slice_in_dim(query_rows, first_block * BLOCK, group_size * BL...]
    another operation x1 -> x0, loops' own time: 10.2 us -> none  [attend_blocks(): lax.map(one_group, jnp.arange(blocks // group_size, dtype=jnp.int32))]
    dynamic_update_slice x16 -> x0, local copies, waits for them, and re-layouts: 6.21 us -> none  [attend_blocks(): lax.map(one_group, jnp.arange(blocks // group_size, dtype=jnp.int32))]
  transfers between devices with their start and end apart: 2 -> 2, of which waited for: 2 -> 2; matrix products, arithmetic and copies ran while one was open for 1% -> 2% of each run, Pallas kernels for 0% -> 0%
where the time goes in v1:
time: 253 us; the launch traced here: 252 us
  waiting for transfers between devices  142 us (56%)
  Pallas kernels  23.7 us (9%)
  matrix products  20.9 us (8%)
  blocking collectives  18.9 us (7%)
  between operations  13.5 us (5%)
  local copies, waits for them, and re-layouts  12.5 us (5%)
  starting transfers between devices  12.3 us (5%)
  other arithmetic  8.93 us (4%)
    all_to_all x1, waiting for transfers between devices, on_device(): lax.all_to_all(outgoing, 'graph', split_axis=0, concat_axis=0, tiled=True)  91.2 us
    all_gather x1, waiting for transfers between devices, on_device(): lax.all_gather(normed, 'attn', axis=0, tiled=True)  50.5 us
    pallas_call x1, Pallas kernels, attend_blocks(): pl.pallas_call(attend_kernel, out_shape=jax.ShapeDtypeStruct((joined.shap...  23.7 us
    all_to_all x1, blocking collectives, on_device(): lax.all_to_all(attended, 'attn', split_axis=0, concat_axis=1, tiled=True)  18.9 us
    all_to_all x1, starting transfers between devices, on_device(): lax.all_to_all(outgoing, 'graph', split_axis=0, concat_axis=0, tiled=True)  12.3 us
    dot_general x1, matrix products, on_device(): jnp.dot(lax.all_gather(normed, 'attn', axis=0, tiled=True), own_columns,...  8.26 us
    gather x1, local copies, waits for them, and re-layouts, aggregate(): jnp.take(source, edge_blocks.reshape(-1), axis=0)  6.95 us
    dot_general x1, matrix products, gather_halo(): jnp.dot(pick, features, preferred_element_type=jnp.float32)  5.2 us
  transfers between devices with their start and end apart: 2, of which 2 were waited for; matrix products, arithmetic and copies ran while one was open for 2% of the time, Pallas kernels for 0%

profile of v1, /device:TPU:1, one launch (start us, length us, event | category | flops | bytes accessed | tf_op | source)
XLA Modules:
  0.0 252.4 jit_solution(17899672316573311455)
XLA Ops:
  6.5 0.0 copy-start
  6.5 0.9 squeeze.7
  7.5 0.7 iota_compare_fusion.4
  8.2 0.1 lt.48
  8.3 5.2 %fusion.4 = bf16[2048,1024]{1,0:T(8,128)(2,1)} fusion(bf16[512,1024]{1,0:T(8,128)(2,1)} %param.11, s32[2048]{0:T(1024)S(1)} %broadcast_select_fusion), kind=kOutput, calls=%fused_computation.8 | convolution fusion | flops 2150629376 | bytes 5251072 | tf_op jit(solution)/shard_map/dot_general | solution.py:21
  13.5 0.0 copy-start.5
  13.5 12.3 %all-to-all-start = ((bf16[32,64,1024]{2,1,0:T(8,128)(2,1)}), bf16[32,64,1024]{2,1,0:T(8,128)(2,1)}, u32[]{:S(2)}, u32[]{:S(2)}) async-start(bf16[32,64,1024]{2,1,0:T(8,128)(2,1)} %bitcast.42), calls=%async_computation | async-start | bytes 8388608 | tf_op jit(solution)/shard_map/all_to_all | solution.py:134
  25.8 0.0 copy-start.1
  25.8 0.0 all-gather.2.cloned.1.call-start
  25.9 0.0 copy-done.5
  25.9 0.1 reshape.105
  26.0 1.6 reduce_sum.18
  27.7 91.2 %all-to-all-done = bf16[32,64,1024]{2,1,0:T(8,128)(2,1)} async-done(((bf16[32,64,1024]{2,1,0:T(8,128)(2,1)}), bf16[32,64,1024]{2,1,0:T(8,128)(2,1)}, u32[]{:S(2)}, u32[]{:S(2)}) %all-to-all-start) | async-done | bytes 4194336 | tf_op jit(solution)/shard_map/all_to_all | solution.py:134
  118.8 0.0 copy-done.1
  118.8 5.2 %pad_maximum_fusion = bf16[2560,1024]{1,0:T(8,128)(2,1)} fusion(bf16[2048,1024]{1,0:T(8,128)(2,1)} %bitcast.4, bf16[512,1024]{1,0:T(8,128)(2,1)S(1)} %copy-done.1), kind=kLoop, calls=%fused_computation.5 | loop fusion | flops 10485760 | bytes 10485760 | tf_op jit(solution)/shard_map/concatenate | solution.py:35
  124.0 6.9 %gather_fusion = bf16[24,128,1024]{2,1,0:T(8,128)(2,1)} fusion(bf16[20,128,1024]{2,1,0:T(8,128)(2,1)} %bitcast.40, s32[1024]{0:T(1024)S(1)} %pad_clamp_fusion), kind=kCustom, calls=%fused_computation | custom fusion | bytes 12583008 | tf_op jit(solution)/shard_map/jit(_take)/gather | solution.py:36
  130.9 0.0 copy-start.6
  130.9 5.2 %fusion.8 = (f32[4,128]{1,0:T(4,128)S(1)}, bf16[4,128,1024]{2,1,0:T(8,128)(2,1)S(1)}) fusion(f32[4,128]{1,0:T(4,128)S(1)} %add_rsqrt_fusion, bf16[4,6,128,1024]{3,2,1,0:T(8,128)(2,1)} %bitcast.41, pred[4,6]{1,0:T(4,128)(4,1)S(1)} %compare_and_fusion, s32[4,6,128,128]{3,2,1,0:T(8,128)} %param.15, bf16[4,128,1024]{2,1,0:T(8,128)(2,1)S(1)} %bitcast.43), kind=kOutput, calls=%fused_computation.16 | convolution fusion | flops 812514816 | bytes 9965592 | tf_op jit(solution)/shard_map/bnij,bnjd->bid/dot_general | solution.py:40
  136.1 0.0 copy-start.2
  136.1 0.0 copy-start.4
  136.1 0.9 copy-done.2
  137.1 0.0 copy-done.6
  137.1 1.4 fusion.10
  138.4 0.0 all-gather.2.cloned.1.call-update
  138.5 0.0 copy-done.4
  138.5 0.1 copy.13
  138.6 1.0 constant_dynamic-slice_fusion.2
  139.5 1.1 constant_dynamic-slice_fusion
  140.6 50.5 %all-gather.2.cloned.1.call-done = bf16[4096,1024]{1,0:T(8,128)(2,1)} async-done(((bf16[512,1024]{1,0:T(8,128)(2,1)}), bf16[4096,1024]{1,0:T(8,128)(2,1)}) %all-gather.2.cloned.1.call-update) | async-done | bytes 8388624 | tf_op jit(solution)/shard_map/all_gather | solution.py:148
  191.1 8.3 %convolution_convert_fusion.joined_ref = bf16[4096,384]{1,0:T(8,128)(2,1)S(1)} fusion(bf16[4096,1024]{1,0:T(8,128)(2,1)} %all-gather.2.cloned.1.call-done, bf16[1024,128]{1,0:T(8,128)(2,1)S(1)} %get-tuple-element.7, bf16[1024,128]{1,0:T(8,128)(2,1)S(1)} %get-tuple-element.8, bf16[1024,128]{1,0:T(8,128)(2,1)S(1)} %constant_dynamic-slice_fusion.2), kind=kOutput, calls=%fused_computation.4 | convolution fusion | flops 3225157632 | bytes 12320768 | tf_op jit(solution)/shard_map/dot_general | solution.py:147
  199.4 23.7 %shard_map.109 = bf16[4096,128]{1,0:T(8,128)(2,1)S(1)} custom-call(s32[32,16]{1,0:T(8,128)S(1)} %bitcast.39, bf16[4096,384]{1,0:T(8,128)(2,1)S(1)} %convolution_convert_fusion.joined_ref), custom_call_target="tpu_custom_call" | custom-call | tf_op jit(solution)/shard_map/pallas_call | solution.py:106
  223.1 1.3 copy.14
  224.4 0.0 copy-start.3
  224.4 18.9 %all_to_all.24 = bf16[8,512,128]{1,2,0:T(8,128)(2,1)S(1)} all-to-all(bf16[8,512,128]{1,2,0:T(8,128)(2,1)} %copy.14), channel_id=1, replica_groups=mesh['graph'=32,'attn'=8] {'attn'}, dimensions={0} | all-to-all | bytes 2097152 | tf_op jit(solution)/shard_map/all_to_all | solution.py:153
  243.3 0.0 copy-done
  243.3 0.0 copy-done.3
  243.3 2.3 fusion.11
  (6 shorter events, 0.0 us)
Async XLA Ops:
  6.5 236.8 %copy-start = (bf16[1024,1024]{1,0:T(8,128)(2,1)S(1)}, bf16[1024,1024]{1,0:T(8,128)(2,1)}, u32[]{:S(2)}) copy-start(bf16[1024,1024]{1,0:T(8,128)(2,1)} %param.21) | copy-start | bytes 6291460
  13.5 12.4 %copy-start.5 = (s32[4,6]{1,0:T(4,128)S(1)}, s32[4,6]{1,0:T(4,128)}, u32[]{:S(2)}) copy-start(s32[4,6]{1,0:T(4,128)} %param.14) | copy-start | bytes 292
  13.5 105.3 %all-to-all-start = ((bf16[32,64,1024]{2,1,0:T(8,128)(2,1)}), bf16[32,64,1024]{2,1,0:T(8,128)(2,1)}, u32[]{:S(2)}, u32[]{:S(2)}) async-start(bf16[32,64,1024]{2,1,0:T(8,128)(2,1)} %bitcast.42), calls=%async_computation | async-start | bytes 8388608 | tf_op jit(solution)/shard_map/all_to_all | solution.py:134
  25.8 93.0 %copy-start.1 = (bf16[512,1024]{1,0:T(8,128)(2,1)S(1)}, bf16[512,1024]{1,0:T(8,128)(2,1)}, u32[]{:S(2)}) copy-start(bf16[512,1024]{1,0:T(8,128)(2,1)} %param.11) | copy-start | bytes 3145732
  25.8 165.3 %all-gather.2.cloned.1.call-start = ((), (), s32[]{:S(2)}) async-start(), calls=%async_computation.2 | async-start | bytes 9437184 | tf_op jit(solution)/shard_map/all_gather | solution.py:148
  130.9 6.1 %copy-start.6 = (f32[1024]{0:T(1024)S(1)}, f32[1024]{0:T(1024)}, u32[]{:S(2)}) copy-start(f32[1024]{0:T(1024)} %param.17) | copy-start | bytes 12292
  136.1 1.0 copy-start.2
  136.1 2.4 copy-start.4
  224.4 18.9 %copy-start.3 = (bf16[4,128,1024]{2,1,0:T(8,128)(2,1)S(1)}, bf16[4,128,1024]{2,1,0:T(8,128)(2,1)}, u32[]{:S(2)}) copy-start(bf16[4,128,1024]{2,1,0:T(8,128)(2,1)} %copy-done.2) | copy-start | bytes 3145732
Sparse Core Ops, SparseCore 0:
  138.6 52.4 all-gather.1

commit v2 on v1

--- a/solution.py
+++ b/solution.py
@@ -7,44 +7,359 @@
 
 HEAD_DIM = 64
 BLOCK = 128
-
-
 EPSILON = 1e-06
-
-
-def gather_halo(features, row_lists, live_counts):
-    groups, slot_count = row_lists.shape
-    row_count = features.shape[0]
-    living = jnp.arange(slot_count, dtype=jnp.int32)[None, :] < live_counts[:, None]
-    chosen = jnp.where(living, row_lists, -1).reshape(-1)
-    pick = (chosen[:, None] == jnp.arange(row_count, dtype=jnp.int32)[None, :]).astype(jnp.bfloat16)
-    picked = jnp.dot(pick, features, preferred_element_type=jnp.float32).astype(jnp.bfloat16)
-    return picked.reshape(groups, slot_count, features.shape[1])
-
-
-def finish(features, summed, edge_weight):
-    row_count, model_width = features.shape
-    degree = jnp.sum(edge_weight, axis=(1, 3)).astype(jnp.float32)
-    own_rows = features.reshape(-1, BLOCK, model_width).astype(jnp.float32)
-    result = (own_rows + summed) * lax.rsqrt(1.0 + degree)[:, :, None]
-    return result.reshape(row_count, model_width).astype(jnp.bfloat16)
-
-
-def aggregate(features, halo, edge_blocks, edge_weight):
-    model_width = features.shape[1]
-    source = jnp.concatenate([features, halo], axis=0).reshape(-1, BLOCK, model_width)
-    picked = jnp.take(source, edge_blocks.reshape(-1), axis=0).reshape(
-        edge_blocks.shape + (BLOCK, model_width)
+NZ = 8
+NY = 4
+NX = 4
+SLOT = 64
+CHUNKS = (256, 256, 256, 256)
+AHEAD = 1
+PLUS = (0, 1)
+MINUS = (2, 3)
+f32 = jnp.float32
+bf16 = jnp.bfloat16
+
+
+def spread_kernel(
+    features, slots, blocks_ref, edges, gain, query_hbm, key_hbm, value_hbm,
+    joined, own_out, *scratch,
+):
+    count = len(CHUNKS)
+    starts = [sum(CHUNKS[:c]) for c in range(count)]
+    scratch = list(scratch)
+    source = [scratch.pop(0) for _ in range(count)]
+    tables = [scratch.pop(0) for _ in range(count)]
+    staged = [scratch.pop(0) for _ in range(count)]
+    gathered = [scratch.pop(0) for _ in range(count)]
+    (
+        slots_in, picks, weights, scale, columns, folded, total, squares,
+        column_sem, slot_send, slot_recv, table_send, table_recv, halo_send, halo_recv,
+        ring_send, ring_recv, pair_send, pair_recv,
+    ) = scratch
+    rows = features.shape[0]
+    own = rows // BLOCK
+    graph = lax.axis_index("graph")
+    attn = lax.axis_index("attn")
+    z, y = graph // NY, graph % NY
+    x, core = attn // 2, attn % 2
+
+    def part(dz, dy=0):
+        return lax.rem(z + dz + NZ, NZ) * NY + lax.rem(y + dy, NY)
+
+    def peer(dx, flip=0):
+        return lax.rem(x + dx + NX, NX) * 2 + (core if flip == 0 else 1 - core)
+
+    def remote(src, dst, send, recv, to):
+        return pltpu.make_async_remote_copy(
+            src_ref=src, dst_ref=dst, send_sem=send, recv_sem=recv,
+            device_id=to, device_id_type=pl.DeviceIdType.MESH,
+        )
+
+    width = 2 * HEAD_DIM
+    first_col = pl.multiple_of(attn * width, width)
+    loads = [
+        pltpu.make_async_copy(
+            ref.at[:, pl.ds(first_col, width)], columns.at[k], column_sem.at[k]
+        )
+        for k, ref in enumerate((query_hbm, key_hbm, value_hbm))
+    ]
+    for load in loads:
+        load.start()
+    for c in range(count):
+        source[c][0:own] = features[:, starts[c] : starts[c] + CHUNKS[c]].reshape(
+            own, BLOCK, CHUNKS[c]
+        )
+
+    barrier = pltpu.get_barrier_semaphore()
+    near = {(0, dy) for dy in range(1, NY)}
+    near |= {(dz, dy) for dz in (1, -1) for dy in range(NY)}
+    for dy in PLUS:
+        near |= {(2, dy), (-2, -dy % NY)}
+    for dy in MINUS:
+        near |= {(-2, dy), (2, -dy % NY)}
+    near = sorted(near)
+    greeted = [(part(dz, dy), attn) for dz, dy in near]
+    greeted += [(graph, peer(1)), (graph, peer(-1)), (graph, peer(0, 1))]
+    for device in greeted:
+        pl.semaphore_signal(barrier, inc=1, device_id=device, device_id_type=pl.DeviceIdType.MESH)
+    pl.semaphore_wait(barrier, len(greeted))
+
+    def go(copy):
+        copy.start()
+
+    ring = [1, -1]
+
+    def slot_copy(k, src):
+        return remote(
+            src, slots_in.at[k], slot_send.at[k], slot_recv.at[k], (part(ring[k % 2]), attn)
+        )
+
+    def table_copy(c, k, src):
+        return remote(
+            src, tables[c].at[k], table_send.at[c, k], table_recv.at[c, k],
+            (part(ring[k % 2]), attn),
+        )
+
+    def send_own(c):
+        for k in range(2):
+            go(table_copy(c, k, source[c].at[0:own]))
+
+    for k in range(2):
+        go(slot_copy(k, slots))
+    for c in range(AHEAD):
+        send_own(c)
+
+    plan = [(0, [(0, dy) for dy in range(NY)])]
+    for side in (1, -1):
+        plan.append((-side, [(0, dy) for dy in range(NY)]))
+    for side, far in ((1, PLUS), (-1, MINUS)):
+        plan.append(
+            (
+                -2 * side,
+                [(0, dy) for dy in range(NY)]
+                + [(side, dy) for dy in range(NY)]
+                + [(2 * side, dy) for dy in far],
+            )
+        )
+    pick_start = [sum(len(p[1]) for p in plan[:k]) * SLOT for k in range(len(plan))]
+    stage_start = [sum(len(p[1]) - 1 for p in plan[:k]) * SLOT for k in range(len(plan))]
+
+    lane = lax.broadcasted_iota(jnp.int32, (SLOT, 128), 1)
+    row_number = lax.broadcasted_iota(jnp.int32, (SLOT, rows), 1).astype(f32)
+
+    def build(k, ref):
+        known = ref[...]
+        for n, (dz, dy) in enumerate(plan[k][1]):
+            wanted = jnp.sum(
+                jnp.where(lane == part(dz, dy), known, 0.0), axis=1, keepdims=True
+            )
+            picks[pick_start[k] + n * SLOT : pick_start[k] + (n + 1) * SLOT, :] = jnp.where(
+                row_number == wanted, 1.0, 0.0
+            ).astype(bf16)
+
+    def halo_rows(sender):
+        low = pl.multiple_of(sender % 2 * SLOT, SLOT)
+        return own + sender // 2, pl.ds(low, SLOT)
+
+    def extract(c, k, table):
+        sender_dz, dests = plan[k]
+        sender = part(sender_dz)
+        size = len(dests) * SLOT
+        found = jnp.dot(
+            picks[pick_start[k] : pick_start[k] + size, :], table, preferred_element_type=f32
+        ).astype(bf16)
+        source[c][(*halo_rows(sender), slice(None))] = found[0:SLOT]
+        at = stage_start[k]
+        staged[c][at : at + size - SLOT, :] = found[SLOT:]
+        for n, (dz, dy) in enumerate(dests[1:]):
+            go(
+                remote(
+                    staged[c].at[at + n * SLOT : at + (n + 1) * SLOT],
+                    source[c].at[halo_rows(sender)],
+                    halo_send.at[c], halo_recv.at[c], (part(dz, dy), attn),
+                )
+            )
+
+    def first_hop(c):
+        extract(c, 0, source[c][0:own].reshape(rows, CHUNKS[c]))
+        for k in range(2):
+            if c == 0:
+                slot_copy(k, slots).wait_recv()
+                go(slot_copy(k + 2, slots_in.at[k]))
+            table_copy(c, k, source[c].at[0:own]).wait_recv()
+            go(table_copy(c, k + 2, tables[c].at[k]))
+        if c + AHEAD < count:
+            send_own(c + AHEAD)
+        for k in range(2):
+            if c == 0:
+                build(k + 1, slots_in.at[k])
+            extract(c, k + 1, tables[c][k].reshape(rows, CHUNKS[c]))
+
+    def second_hop(c):
+        for k in range(2, 4):
+            if c == 0:
+                slot_copy(k, slots).wait_recv()
+                build(k + 1, slots_in.at[k])
+            table_copy(c, k, source[c].at[0:own]).wait_recv()
+            extract(c, k + 1, tables[c][k].reshape(rows, CHUNKS[c]))
+
+    def slot_rows(owner, low=0, high=None):
+        high = rows if high is None else high
+        return pl.ds(pl.multiple_of(owner * rows + low, BLOCK), high - low)
+
+    half = rows // 2
+    pieces = [(0, 0, rows), (0, 0, rows), (-1, 0, half), (1, half, rows)]
+
+    def ring_copy(c, k):
+        dx, low, high = pieces[k]
+        at = gathered[c].at[slot_rows(peer(dx), low, high)]
+        return remote(at, at, ring_send.at[c, k], ring_recv.at[c, k], (graph, peer(ring[k % 2])))
+
+    def pair_copy(c, k):
+        at = gathered[c].at[slot_rows(peer((0, -1, 1, 2)[k]))]
+        return remote(at, at, pair_send.at[c, k], pair_recv.at[c, k], (graph, peer(0, 1)))
+
+    def blend(c):
+        remote(
+            staged[c], staged[c],
+            halo_send.at[c], halo_recv.at[c], (graph, peer(0, 1)),
+        ).wait_recv()
+        for b in range(rows // BLOCK):
+            chosen = [source[c][blocks_ref[b, n]] for n in range(blocks_ref.shape[1])]
+            here = slice(b * BLOCK, (b + 1) * BLOCK)
+            mixed = jnp.dot(
+                weights[here, :], jnp.concatenate(chosen, axis=0), preferred_element_type=f32
+            )
+            mixed = mixed + source[c][b].astype(f32)
+            mixed = (mixed * scale[here, 0:1]).astype(bf16)
+            own_out[here, starts[c] : starts[c] + CHUNKS[c]] = mixed
+            gathered[c][
+                pl.ds(pl.multiple_of(attn * rows + b * BLOCK, BLOCK), BLOCK), :
+            ] = mixed
+        go(ring_copy(c, 0))
+        go(ring_copy(c, 1))
+        go(pair_copy(c, 0))
+
+    def pass_on(c):
+        for k in range(2):
+            ring_copy(c, k).wait_recv()
+            go(ring_copy(c, k + 2))
+            go(pair_copy(c, k + 1))
+
+    def pass_last(c):
+        for k in range(2, 4):
+            ring_copy(c, k).wait_recv()
+        go(pair_copy(c, 3))
+
+    def project(c):
+        for k in range(4):
+            pair_copy(c, k).wait_recv()
+
+        def one(owner, carry):
+            at = slot_rows(owner)
+            values = gathered[c][at, :]
+            made = jnp.dot(
+                values, folded[starts[c] : starts[c] + CHUNKS[c], :], preferred_element_type=f32
+            )
+            wide = values.astype(f32)
+            wide = wide * wide
+            squared = sum(wide[:, i : i + 128] for i in range(0, CHUNKS[c], 128))
+            if c > 0:
+                made = made + total[at, :]
+                squared = squared + squares[at, :]
+            if c + 1 < count:
+                total[at, :] = made
+                squares[at, :] = squared
+            else:
+                mean = jnp.sum(squared, axis=1, keepdims=True) * (1.0 / sum(CHUNKS))
+                joined[at, :] = (made * lax.rsqrt(mean + EPSILON)).astype(bf16)
+            return carry
+
+        lax.fori_loop(0, 2 * NX, one, 0)
+
+    build(0, slots)
+    for c in range(count):
+        first_hop(c)
+        if c == 0:
+            for b in range(edges.shape[0]):
+                here = slice(b * BLOCK, (b + 1) * BLOCK)
+                degree = jnp.zeros((BLOCK, BLOCK), f32)
+                for n in range(edges.shape[1]):
+                    value = edges[b, n].astype(f32)
+                    degree = degree + value
+                    weights[here, n * BLOCK : (n + 1) * BLOCK] = value.astype(bf16)
+                degree = jnp.sum(degree, axis=1, keepdims=True)
+                scale[here, :] = jnp.broadcast_to(lax.rsqrt(1.0 + degree), (BLOCK, BLOCK))
+            for k, load in enumerate(loads):
+                load.wait()
+                folded[:, k * width : (k + 1) * width] = (
+                    columns[k].astype(f32) * gain[...]
+                ).astype(bf16)
+        if c >= 2:
+            pass_last(c - 2)
+        if c >= 1:
+            blend(c - 1)
+        if c >= 2:
+            project(c - 2)
+        second_hop(c)
+        if c >= 1:
+            pass_on(c - 1)
+    if count >= 2:
+        pass_last(count - 2)
+    blend(count - 1)
+    if count >= 2:
+        project(count - 2)
+    pass_on(count - 1)
+    pass_last(count - 1)
+    project(count - 1)
+
+    for k in range(4):
+        slot_copy(k, slots).wait_send()
+    for c in range(count):
+        for k in range(4):
+            table_copy(c, k, source[c].at[0:own]).wait_send()
+            ring_copy(c, k).wait_send()
+            pair_copy(c, k).wait_send()
+        remote(
+            staged[c], staged[c],
+            halo_send.at[c], halo_recv.at[c], (graph, peer(0, 1)),
+        ).wait_send()
+
+
+def spread(features, slots, edge_blocks, edge_weight, gain, query_weight, key_weight, value_weight):
+    rows, model = features.shape
+    members = 2 * NX
+    width = 2 * HEAD_DIM
+    nb = edge_blocks.shape[1]
+    count = len(CHUNKS)
+    vmem = pl.BlockSpec(memory_space=pltpu.VMEM)
+    smem = pl.BlockSpec(memory_space=pltpu.SMEM)
+    hbm = pl.BlockSpec(memory_space=pl.ANY)
+    arriving = (NZ * NY - 5) * SLOT
+    own = rows // BLOCK
+    sources = own + NZ * NY * SLOT // BLOCK
+    scratch = [pltpu.VMEM((sources, BLOCK, w), bf16) for w in CHUNKS]
+    scratch += [pltpu.VMEM((4, own, BLOCK, w), bf16) for w in CHUNKS]
+    scratch += [pltpu.VMEM((arriving, w), bf16) for w in CHUNKS]
+    scratch += [pltpu.VMEM((members * rows, w), bf16) for w in CHUNKS]
+    scratch += [
+        pltpu.VMEM((4, SLOT, 128), f32),
+        pltpu.VMEM((NZ * NY * SLOT, rows), bf16),
+        pltpu.VMEM((rows, nb * BLOCK), bf16),
+        pltpu.VMEM((rows, BLOCK), f32),
+        pltpu.VMEM((3, model, width), bf16),
+        pltpu.VMEM((model, 3 * width), bf16),
+        pltpu.VMEM((members * rows, 3 * width), f32),
+        pltpu.VMEM((members * rows, 128), f32),
+        pltpu.SemaphoreType.DMA((3,)),
+        pltpu.SemaphoreType.DMA((4,)),
+        pltpu.SemaphoreType.DMA((4,)),
+        pltpu.SemaphoreType.DMA((count, 4)),
+        pltpu.SemaphoreType.DMA((count, 4)),
+        pltpu.SemaphoreType.DMA((count,)),
+        pltpu.SemaphoreType.DMA((count,)),
+        pltpu.SemaphoreType.DMA((count, 4)),
+        pltpu.SemaphoreType.DMA((count, 4)),
+        pltpu.SemaphoreType.DMA((count, 4)),
+        pltpu.SemaphoreType.DMA((count, 4)),
+    ]
+    return pl.pallas_call(
+        spread_kernel,
+        out_shape=(
+            jax.ShapeDtypeStruct((members * rows, 3 * width), bf16),
+            jax.ShapeDtypeStruct((rows, model), bf16),
+        ),
+        in_specs=[vmem, vmem, smem, vmem, vmem, hbm, hbm, hbm],
+        out_specs=(vmem, vmem),
+        scratch_shapes=scratch,
+        compiler_params=pltpu.CompilerParams(
+            collective_id=1, has_side_effects=True, vmem_limit_bytes=58 * 2**20
+        ),
+        name="spread",
+    )(
+        features, slots, edge_blocks, edge_weight, gain.reshape(model, 1),
+        query_weight, key_weight, value_weight,
     )
-    weights = edge_weight.astype(jnp.bfloat16)
-    summed = jnp.einsum("bnij,bnjd->bid", weights, picked, preferred_element_type=jnp.float32)
-    return finish(features, summed, edge_weight)
-
-
-def normalize(aggregated, norm_gain):
-    values = aggregated.astype(jnp.float32)
-    scaled = values * lax.rsqrt(jnp.mean(values * values, axis=1, keepdims=True) + EPSILON)
-    return (scaled * norm_gain).astype(jnp.bfloat16)
 
 
 def attend_kernel(mask_ref, joined_ref, out_ref, scores_a, scores_b):
@@ -129,32 +444,16 @@
     value_weight,
     out_weight,
 ):
-    outgoing = gather_halo(features, send_rows[0], send_count[0])
-    model_width = features.shape[1]
-    incoming = lax.all_to_all(outgoing, "graph", split_axis=0, concat_axis=0, tiled=True)
-    halo = incoming.reshape(-1, model_width)
-    aggregated = aggregate(features, halo, edge_blocks, edge_weight)
-    normed = normalize(aggregated, norm_gain)
-    head_width = query_weight.shape[1] // lax.axis_size("attn")
-    first_col = lax.axis_index("attn") * head_width
-    own_columns = jnp.concatenate(
-        [
-            lax.dynamic_slice_in_dim(matrix, first_col, head_width, 1)
-            for matrix in (query_weight, key_weight, value_weight)
-        ],
-        axis=1,
+    slot = jnp.arange(SLOT, dtype=jnp.int32)[:, None]
+    slots = jnp.where(slot < send_count, send_rows[0].T, -1).astype(f32)
+    slots = jnp.pad(slots, ((0, 0), (0, 128 - slots.shape[1])))
+    joined, aggregated = spread(
+        features, slots, edge_blocks, edge_weight, norm_gain, query_weight, key_weight, value_weight
     )
-    joined = jnp.dot(
-        lax.all_gather(normed, "attn", axis=0, tiled=True),
-        own_columns,
-        preferred_element_type=jnp.float32,
-    ).astype(jnp.bfloat16)
     attended = attend_blocks(joined, mask_blocks[0])
     returned = lax.all_to_all(attended, "attn", split_axis=0, concat_axis=1, tiled=True)
-    updated = jnp.dot(returned, out_weight, preferred_element_type=jnp.float32) + aggregated.astype(
-        jnp.float32
-    )
-    return updated.astype(jnp.bfloat16)
+    updated = jnp.dot(returned, out_weight, preferred_element_type=f32) + aggregated.astype(f32)
+    return updated.astype(bf16)
 
 
 def solution(mesh):

time: 253 us -> 160 us (0.63)
  waiting for transfers between devices: 142 us -> 0 us
  Pallas kernels: 23.7 us -> 130 us
  matrix products: 20.9 us -> 2.27 us
  between operations: 13.5 us -> 0.03 us
  starting transfers between devices: 12.3 us -> 0 us
  other arithmetic: 8.93 us -> 0.66 us
  local copies, waits for them, and re-layouts: 12.5 us -> 7.24 us
    pallas_call x0 -> x1, Pallas kernels: none -> 106 us  [spread(): pl.pallas_call(spread_kernel, out_shape=(jax.ShapeDtypeStruct((members *...]
    all_to_all x1 -> x0, waiting for transfers between devices: 91.2 us -> none  [on_device(): lax.all_to_all(outgoing, 'graph', split_axis=0, concat_axis=0, tiled=True)]
    all_gather x1 -> x0, waiting for transfers between devices: 50.5 us -> none  [on_device(): lax.all_gather(normed, 'attn', axis=0, tiled=True)]
    dot_general x4 -> x1, matrix products: 20.9 us -> 2.27 us  [on_device(): jnp.dot(returned, out_weight, preferred_element_type=f32)]
    all_to_all x1 -> x0, starting transfers between devices: 12.3 us -> none  [on_device(): lax.all_to_all(outgoing, 'graph', split_axis=0, concat_axis=0, tiled=True)]
    gather x1 -> x0, local copies, waits for them, and re-layouts: 6.95 us -> none  [aggregate(): jnp.take(source, edge_blocks.reshape(-1), axis=0)]
    concatenate x1 -> x0, other arithmetic: 5.15 us -> none  [aggregate(): jnp.concatenate([features, halo], axis=0).reshape(-1, BLOCK, model_width)]
    unnamed x15 -> x8, local copies, waits for them, and re-layouts: 1.05 us -> 3.61 us
  transfers between devices with their start and end apart: 2 -> 0, of which waited for: 2 -> 0; matrix products, arithmetic and copies ran while one was open for 2% -> 0% of each run, Pallas kernels for 0% -> 0%
where the time goes in v2:
time: 160 us
  Pallas kernels  130 us (81%)
  blocking collectives  19.8 us (12%)
  local copies, waits for them, and re-layouts  7.24 us (5%)
  matrix products  2.27 us (1%)
    pallas_call x1, Pallas kernels, spread(): pl.pallas_call(spread_kernel, out_shape=(jax.ShapeDtypeStruct((members *...  106 us
    pallas_call x1, Pallas kernels, attend_blocks(): pl.pallas_call(attend_kernel, out_shape=jax.ShapeDtypeStruct((joined.shap...  23.7 us
    all_to_all x1, blocking collectives, on_device(): lax.all_to_all(attended, 'attn', split_axis=0, concat_axis=1, tiled=True)  19.8 us
    unnamed x8, local copies, waits for them, and re-layouts  3.61 us

profile of v2, /device:TPU:1, one launch (start us, length us, event | category | flops | bytes accessed | tf_op | source)
XLA Modules:
  0.0 159.6 jit_solution(9790893384586194165)
XLA Ops:
  0.0 0.0 copy-start
  0.0 0.9 copy.14
  0.9 0.8 copy.15
  1.7 1.7 %copy.16.gain = f32[1024,1]{1,0:T(8,128)} copy(f32[1024,1]{0,1:T(1,128)} %bitcast.18) | data formatting | bytes 8192 | tf_op jit(solution)/shard_map/reshape | solution.py:360
  3.4 0.7 fusion
  4.1 0.6 pad.4.slots
  4.7 105.9 %spread.1 = (bf16[4096,384]{1,0:T(8,128)(2,1)}, bf16[512,1024]{1,0:T(8,128)(2,1)}) custom-call(bf16[512,1024]{1,0:T(8,128)(2,1)} %features.1, f32[64,128]{1,0:T(8,128)} %pad.4.slots, s32[4,6]{1,0:T(4,128)} %blocks_ref.1, s32[4,6,128,128]{3,2,1,0:T(8,128)} %edges.1, f32[1024,1]{1,0:T(8,128)} %copy.16.gain, bf16[1024,1024]{1,0:T(8,128)(2,1)} %query_hbm.1, ...), custom_call_target="tpu_custom_call" | custom-call | tf_op jit(solution)/shard_map/spread/pallas_call | solution.py:346
  110.6 0.0 copy-start.1
  110.6 1.9 %copy-done.1 = bf16[4096,384]{1,0:T(8,128)(2,1)S(1)} copy-done((bf16[4096,384]{1,0:T(8,128)(2,1)S(1)}, bf16[4096,384]{1,0:T(8,128)(2,1)}, u32[]{:S(2)}) %copy-start.1) | copy-done | bytes 3145752
  112.5 23.7 %shard_map.109 = bf16[4096,128]{1,0:T(8,128)(2,1)S(1)} custom-call(s32[32,16]{1,0:T(8,128)S(1)} %bitcast.16, bf16[4096,384]{1,0:T(8,128)(2,1)S(1)} %copy-done.1), custom_call_target="tpu_custom_call" | custom-call | tf_op jit(solution)/shard_map/pallas_call | solution.py:421
  136.2 1.3 copy.17
  137.5 0.0 copy-start.2
  137.5 19.8 %all_to_all.19 = bf16[8,512,128]{1,2,0:T(8,128)(2,1)S(1)} all-to-all(bf16[8,512,128]{1,2,0:T(8,128)(2,1)} %copy.17), channel_id=1, replica_groups=mesh['graph'=32,'attn'=8] {'attn'}, dimensions={0} | all-to-all | bytes 2097152 | tf_op jit(solution)/shard_map/all_to_all | solution.py:454
  157.3 0.0 copy-done
  157.3 0.0 copy-done.2
  157.3 2.3 %add_convert_fusion = bf16[512,1024]{1,0:T(8,128)(2,1)} fusion(bf16[512,1024]{1,0:T(8,128)(2,1)S(1)} %copy-done.2, bf16[512,1024]{0,1:T(8,128)(2,1)S(1)} %bitcast.17, bf16[1024,1024]{1,0:T(8,128)(2,1)S(1)} %copy-done), kind=kOutput, calls=%fused_computation | convolution fusion | flops 1075314688 | bytes 5242880 | tf_op jit(solution)/shard_map/dot_general | solution.py:455
Async XLA Ops:
  0.0 157.3 %copy-start = (bf16[1024,1024]{1,0:T(8,128)(2,1)S(1)}, bf16[1024,1024]{1,0:T(8,128)(2,1)}, u32[]{:S(2)}) copy-start(bf16[1024,1024]{1,0:T(8,128)(2,1)} %param.21) | copy-start | bytes 6291460
  110.6 1.9 %copy-start.1 = (bf16[4096,384]{1,0:T(8,128)(2,1)S(1)}, bf16[4096,384]{1,0:T(8,128)(2,1)}, u32[]{:S(2)}) copy-start(bf16[4096,384]{1,0:T(8,128)(2,1)} %get-tuple-element.7.joined_ref) | copy-start | bytes 9437188
  137.5 19.8 %copy-start.2 = (bf16[512,1024]{1,0:T(8,128)(2,1)S(1)}, bf16[512,1024]{1,0:T(8,128)(2,1)}, u32[]{:S(2)}) copy-start(bf16[512,1024]{1,0:T(8,128)(2,1)} %get-tuple-element.8) | copy-start | bytes 3145732

commit v3 on v2

v3 whole, which is shorter than its diff:
```python
import jax
import jax.numpy as jnp
from jax import lax
from jax.experimental import pallas as pl
from jax.experimental.pallas import tpu as pltpu
from jax.sharding import PartitionSpec as P

HEAD_DIM = 64
BLOCK = 128
EPSILON = 1e-06
SCORE_SCALE = HEAD_DIM ** (-0.5) * 1.4426950408889634
NZ = 8
NY = 4
NX = 4
SLOT = 64
CHUNKS = (256, 256, 256, 256)
AHEAD = 1
PLUS = (0, 1)
MINUS = (2, 3)
f32 = jnp.float32
bf16 = jnp.bfloat16


def layer_kernel(
    features, send_rows, send_count, blocks_ref, mask_ref, gain, edges_hbm,
    query_hbm, key_hbm, value_hbm, out_hbm, result, *scratch,
):
    count = len(CHUNKS)
    starts = [sum(CHUNKS[:c]) for c in range(count)]
    scratch = list(scratch)
    source = [scratch.pop(0) for _ in range(count)]
    tables = [scratch.pop(0) for _ in range(count)]
    staged = [scratch.pop(0) for _ in range(count)]
    gathered = [scratch.pop(0) for _ in range(count)]
    (
        feature_sem, slots, slots_in, edges, picks, weights, scale, columns, folded, out_weight, total, squares,
        own_out, joined, scores_a, scores_b, mixed_out, mixed_in,
        column_sem, mixed_send, mixed_recv, slot_send, slot_recv, table_send, table_recv, halo_send, halo_recv,
        ring_send, ring_recv, pair_send, pair_recv,
    ) = scratch
    own = features.shape[0]
    rows = own * BLOCK
    graph = lax.axis_index("graph")
    attn = lax.axis_index("attn")
    z, y = graph // NY, graph % NY
    x, core = attn // 2, attn % 2

    def part(dz, dy=0):
        return lax.rem(z + dz + NZ, NZ) * NY + lax.rem(y + dy, NY)

    def peer(dx, flip=0):
        return lax.rem(x + dx + NX, NX) * 2 + (core if flip == 0 else 1 - core)

    def remote(src, dst, send, recv, to):
        return pltpu.make_async_remote_copy(
            src_ref=src, dst_ref=dst, send_sem=send, recv_sem=recv,
            device_id=to, device_id_type=pl.DeviceIdType.MESH,
        )

    width = 2 * HEAD_DIM
    first_col = pl.multiple_of(attn * width, width)
    loads = [
        pltpu.make_async_copy(
            ref.at[:, pl.ds(first_col, width)], columns.at[k], column_sem.at[k]
        )
        for k, ref in enumerate((query_hbm, key_hbm, value_hbm))
    ]
    loads.append(pltpu.make_async_copy(edges_hbm, edges, column_sem.at[3]))
    loads.append(pltpu.make_async_copy(out_hbm, out_weight, column_sem.at[4]))
    feature_loads = [
        pltpu.make_async_copy(
            features.at[:, :, pl.ds(starts[c], CHUNKS[c])], source[c].at[0:own], feature_sem.at[c]
        )
        for c in range(count)
    ]
    for load in feature_loads + loads:
        load.start()
    barrier = pltpu.get_barrier_semaphore()
    near = {(0, dy) for dy in range(1, NY)}
    near |= {(dz, dy) for dz in (1, -1) for dy in range(NY)}
    for dy in PLUS:
        near |= {(2, dy), (-2, -dy % NY)}
    for dy in MINUS:
        near |= {(-2, dy), (2, -dy % NY)}
    near = sorted(near)
    greeted = [(part(dz, dy), attn) for dz, dy in near]
    greeted += [(graph, peer(1)), (graph, peer(-1)), (graph, peer(0, 1))]
    greeted += [(graph, peer(2)), (graph, peer(1, 1)), (graph, peer(-1, 1)), (graph, peer(2, 1))]
    for device in greeted:
        pl.semaphore_signal(barrier, inc=1, device_id=device, device_id_type=pl.DeviceIdType.MESH)
    slots[...] = jnp.full((BLOCK, BLOCK), -1.0, f32)
    slots[0 : NZ * NY, 0:SLOT] = send_rows[...].astype(f32)
    turned = slots[...].T
    slots[...] = jnp.zeros((BLOCK, BLOCK), f32)
    slots[0:1, 0 : NZ * NY] = send_count[...].astype(f32)
    place = lax.broadcasted_iota(jnp.int32, (BLOCK, BLOCK), 0).astype(f32)
    slots[...] = jnp.where(place < slots[0:1, :], turned, -1.0)
    pl.semaphore_wait(barrier, len(greeted))

    def go(copy):
        copy.start()

    ring = [1, -1]

    def slot_copy(k, src):
        return remote(
            src, slots_in.at[k], slot_send.at[k], slot_recv.at[k], (part(ring[k % 2]), attn)
        )

    def table_copy(c, k, src):
        return remote(
            src, tables[c].at[k], table_send.at[c, k], table_recv.at[c, k],
            (part(ring[k % 2]), attn),
        )

    def send_own(c):
        feature_loads[c].wait()
        for k in range(2):
            go(table_copy(c, k, source[c].at[0:own]))

    for k in range(2):
        go(slot_copy(k, slots.at[0:SLOT]))
    for c in range(AHEAD):
        send_own(c)

    plan = [(0, [(0, dy) for dy in range(NY)])]
    for side in (1, -1):
        plan.append((-side, [(0, dy) for dy in range(NY)]))
    for side, far in ((1, PLUS), (-1, MINUS)):
        plan.append(
            (
                -2 * side,
                [(0, dy) for dy in range(NY)]
                + [(side, dy) for dy in range(NY)]
                + [(2 * side, dy) for dy in far],
            )
        )
    pick_start = [sum(len(p[1]) for p in plan[:k]) * SLOT for k in range(len(plan))]
    stage_start = [sum(len(p[1]) - 1 for p in plan[:k]) * SLOT for k in range(len(plan))]

    lane = lax.broadcasted_iota(jnp.int32, (SLOT, 128), 1)
    row_number = lax.broadcasted_iota(jnp.int32, (SLOT, rows), 1).astype(f32)

    def build(k, ref):
        known = ref[...]
        for n, (dz, dy) in enumerate(plan[k][1]):
            wanted = jnp.sum(
                jnp.where(lane == part(dz, dy), known, 0.0), axis=1, keepdims=True
            )
            picks[pick_start[k] + n * SLOT : pick_start[k] + (n + 1) * SLOT, :] = jnp.where(
                row_number == wanted, 1.0, 0.0
            ).astype(bf16)

    def halo_rows(sender):
        low = pl.multiple_of(sender % 2 * SLOT, SLOT)
        return own + sender // 2, pl.ds(low, SLOT)

    def extract(c, k, table):
        sender_dz, dests = plan[k]
        sender = part(sender_dz)
        size = len(dests) * SLOT
        found = jnp.dot(
            picks[pick_start[k] : pick_start[k] + size, :], table, preferred_element_type=f32
        ).astype(bf16)
        source[c][(*halo_rows(sender), slice(None))] = found[0:SLOT]
        at = stage_start[k]
        staged[c][at : at + size - SLOT, :] = found[SLOT:]
        for n, (dz, dy) in enumerate(dests[1:]):
            go(
                remote(
                    staged[c].at[at + n * SLOT : at + (n + 1) * SLOT],
                    source[c].at[halo_rows(sender)],
                    halo_send.at[c], halo_recv.at[c], (part(dz, dy), attn),
                )
            )

    def first_hop(c):
        extract(c, 0, source[c][0:own].reshape(rows, CHUNKS[c]))
        for k in range(2):
            if c == 0:
                slot_copy(k, slots.at[0:SLOT]).wait_recv()
                go(slot_copy(k + 2, slots_in.at[k]))
            table_copy(c, k, source[c].at[0:own]).wait_recv()
            go(table_copy(c, k + 2, tables[c].at[k]))
        if c + AHEAD < count:
            send_own(c + AHEAD)
        for k in range(2):
            if c == 0:
                build(k + 1, slots_in.at[k])
            extract(c, k + 1, tables[c][k].reshape(rows, CHUNKS[c]))

    def second_hop(c):
        for k in range(2, 4):
            if c == 0:
                slot_copy(k, slots.at[0:SLOT]).wait_recv()
                build(k + 1, slots_in.at[k])
            table_copy(c, k, source[c].at[0:own]).wait_recv()
            extract(c, k + 1, tables[c][k].reshape(rows, CHUNKS[c]))

    def slot_rows(owner, low=0, high=None):
        high = rows if high is None else high
        return pl.ds(pl.multiple_of(owner * rows + low, BLOCK), high - low)

    half = rows // 2
    pieces = [(0, 0, rows), (0, 0, rows), (-1, 0, half), (1, half, rows)]

    def ring_copy(c, k):
        dx, low, high = pieces[k]
        at = gathered[c].at[slot_rows(peer(dx), low, high)]
        return remote(at, at, ring_send.at[c, k], ring_recv.at[c, k], (graph, peer(ring[k % 2])))

    def pair_copy(c, k):
        at = gathered[c].at[slot_rows(peer((0, -1, 1, 2)[k]))]
        return remote(at, at, pair_send.at[c, k], pair_recv.at[c, k], (graph, peer(0, 1)))

    def blend(c):
        remote(
            staged[c], staged[c],
            halo_send.at[c], halo_recv.at[c], (graph, peer(0, 1)),
        ).wait_recv()
        for b in range(rows // BLOCK):
            chosen = [source[c][blocks_ref[b, n]] for n in range(blocks_ref.shape[1])]
            here = slice(b * BLOCK, (b + 1) * BLOCK)
            mixed = jnp.dot(
                weights[here, :], jnp.concatenate(chosen, axis=0), preferred_element_type=f32
            )
            mixed = mixed + source[c][b].astype(f32)
            mixed = (mixed * scale[here, 0:1]).astype(bf16)
            own_out[here, starts[c] : starts[c] + CHUNKS[c]] = mixed
            gathered[c][
                pl.ds(pl.multiple_of(attn * rows + b * BLOCK, BLOCK), BLOCK), :
            ] = mixed
        go(ring_copy(c, 0))
        go(ring_copy(c, 1))
        go(pair_copy(c, 0))

    def pass_on(c):
        for k in range(2):
            ring_copy(c, k).wait_recv()
            go(ring_copy(c, k + 2))
            go(pair_copy(c, k + 1))

    def pass_last(c):
        for k in range(2, 4):
            ring_copy(c, k).wait_recv()
        go(pair_copy(c, 3))

    def project(c):
        for k in range(4):
            pair_copy(c, k).wait_recv()

        def one(owner, carry):
            at = slot_rows(owner)
            values = gathered[c][at, :]
            made = jnp.dot(
                values, folded[starts[c] : starts[c] + CHUNKS[c], :], preferred_element_type=f32
            )
            wide = values.astype(f32)
            wide = wide * wide
            squared = sum(wide[:, i : i + 128] for i in range(0, CHUNKS[c], 128))
            if c > 0:
                made = made + total[at, :]
                squared = squared + squares[at, :]
            if c + 1 < count:
                total[at, :] = made
                squares[at, :] = squared
            else:
                mean = jnp.sum(squared, axis=1, keepdims=True) * (1.0 / sum(CHUNKS))
                made = (made * lax.rsqrt(mean + EPSILON)).astype(bf16)
                for k in range(3):
                    joined[k, pl.ds(owner * own, own)] = made[
                        :, k * width : (k + 1) * width
                    ].reshape(own, BLOCK, width)
            return carry

        lax.fori_loop(0, 2 * NX, one, 0)

    build(0, slots.at[0:SLOT])
    for c in range(count):
        first_hop(c)
        if c == 0:
            loads[3].wait()
            for b in range(edges.shape[0]):
                here = slice(b * BLOCK, (b + 1) * BLOCK)
                degree = jnp.zeros((BLOCK, BLOCK), f32)
                for n in range(edges.shape[1]):
                    value = edges[b, n].astype(f32)
                    degree = degree + value
                    weights[here, n * BLOCK : (n + 1) * BLOCK] = value.astype(bf16)
                degree = jnp.sum(degree, axis=1, keepdims=True)
                scale[here, :] = jnp.broadcast_to(lax.rsqrt(1.0 + degree), (BLOCK, BLOCK))
            for load in loads[:3]:
                load.wait()
            for i in range(gain.shape[0]):
                here = slice(i * 128, (i + 1) * 128)
                factor = jnp.broadcast_to(gain[i : i + 1, :], (128, 128)).T
                for k in range(3):
                    raised = factor * SCORE_SCALE if k == 0 else factor
                    folded[here, k * width : (k + 1) * width] = (
                        columns[k, here, :].astype(f32) * raised
                    ).astype(bf16)
        if c >= 2:
            pass_last(c - 2)
        if c >= 1:
            blend(c - 1)
        if c >= 2:
            project(c - 2)
        second_hop(c)
        if c >= 1:
            pass_on(c - 1)
    if count >= 2:
        pass_last(count - 2)
    blend(count - 1)
    if count >= 2:
        project(count - 2)
    pass_on(count - 1)
    pass_last(count - 1)
    project(count - 1)

    first = lax.broadcasted_iota(jnp.int32, (BLOCK, width), 1) < HEAD_DIM
    ones = jnp.ones((2 * BLOCK, width), bf16)
    keys = mask_ref.shape[0]

    def pair(block, step, kind):
        low = joined[kind, mask_ref[2 * step, block]]
        high = joined[kind, mask_ref[2 * step + 1, block]]
        return jnp.concatenate([low, high], axis=0)

    def score(block, scores):
        query = joined[0, block]
        zero = jnp.zeros_like(query)
        query = jnp.concatenate(
            [jnp.where(first, query, zero), jnp.where(first, zero, query)], axis=0
        )
        top = None
        for step in range(keys // 2):
            piece = lax.dot_general(
                query, pair(block, step, 1), (((1,), (1,)), ((), ())), preferred_element_type=f32
            )
            scores[:, 2 * step * BLOCK : (2 * step + 2) * BLOCK] = piece
            piece = jnp.maximum(piece[:, :BLOCK], piece[:, BLOCK:])
            top = piece if top is None else jnp.maximum(top, piece)
        return jnp.max(top, axis=1, keepdims=True)

    def mix(block, scores, top):
        sums = jnp.zeros((2 * BLOCK, 2 * width), f32)
        for step in range(keys // 2):
            values = jnp.concatenate([pair(block, step, 2), ones], axis=1)
            piece = scores[:, 2 * step * BLOCK : (2 * step + 2) * BLOCK]
            raised = jnp.exp2(piece - top).astype(bf16)
            sums = sums + jnp.dot(raised, values, preferred_element_type=f32)
        sums = sums[:, :width] / sums[:, width:]
        return jnp.where(first, sums[:BLOCK], sums[BLOCK:]).astype(bf16)

    def mixed_copy(owner, low):
        return remote(
            mixed_out.at[pl.ds(pl.multiple_of(owner * rows + low, BLOCK), 2 * BLOCK)],
            mixed_in.at[attn, pl.ds(pl.multiple_of(low, BLOCK), 2 * BLOCK)],
            mixed_send, mixed_recv, (graph, owner),
        )

    def attend(index):
        owner = lax.rem(attn + 1 + index // 2, 2 * NX)
        low = lax.rem(index, 2) * (2 * BLOCK)
        block = owner * own + lax.rem(index, 2) * 2
        top_a = score(block, scores_a)
        top_b = score(block + 1, scores_b)
        low_rows = mix(block, scores_a, top_a)
        high_rows = mix(block + 1, scores_b, top_b)
        return owner, low, low_rows, high_rows

    def away(index, carry):
        owner, low, low_rows, high_rows = attend(index)
        at = pl.multiple_of(owner * rows + low, BLOCK)
        mixed_out[pl.ds(at, BLOCK), :] = low_rows
        mixed_out[pl.ds(pl.multiple_of(at + BLOCK, BLOCK), BLOCK), :] = high_rows
        mixed_copy(owner, low).start()
        return carry

    def home(index, carry):
        owner, low, low_rows, high_rows = attend(index)
        at = pl.multiple_of(low, BLOCK)
        mixed_in[attn, pl.ds(at, BLOCK), :] = low_rows
        mixed_in[attn, pl.ds(pl.multiple_of(at + BLOCK, BLOCK), BLOCK), :] = high_rows
        return carry

    lax.fori_loop(0, 4 * NX - 2, away, 0)
    lax.fori_loop(4 * NX - 2, 4 * NX, home, 0)
    returned = remote(
        mixed_out.at[0 : (2 * NX - 1) * rows], mixed_out.at[0 : (2 * NX - 1) * rows],
        mixed_send, mixed_recv, (graph, peer(0, 1)),
    )
    loads[4].wait()
    returned.wait_recv()
    for b in range(own):
        here = slice(b * BLOCK, (b + 1) * BLOCK)
        attended = jnp.concatenate([mixed_in[k, here, :] for k in range(2 * NX)], axis=1)
        made = jnp.dot(attended, out_weight[...], preferred_element_type=f32)
        result[here, :] = (made + own_out[here, :].astype(f32)).astype(bf16)

    returned.wait_send()
    for k in range(4):
        slot_copy(k, slots.at[0:SLOT]).wait_send()
    for c in range(count):
        for k in range(4):
            table_copy(c, k, source[c].at[0:own]).wait_send()
            ring_copy(c, k).wait_send()
            pair_copy(c, k).wait_send()
        remote(
            staged[c], staged[c],
            halo_send.at[c], halo_recv.at[c], (graph, peer(0, 1)),
        ).wait_send()


def on_device(
    features,
    send_rows,
    send_count,
    edge_blocks,
    edge_weight,
    mask_blocks,
    norm_gain,
    query_weight,
    key_weight,
    value_weight,
    out_weight,
):
    rows, model = features.shape
    members = 2 * NX
    width = 2 * HEAD_DIM
    keys = mask_blocks.shape[2] * BLOCK
    nb = edge_blocks.shape[1]
    count = len(CHUNKS)
    own = rows // BLOCK
    sources = own + NZ * NY * SLOT // BLOCK
    arriving = (NZ * NY - 5) * SLOT
    vmem = pl.BlockSpec(memory_space=pltpu.VMEM)
    smem = pl.BlockSpec(memory_space=pltpu.SMEM)
    hbm = pl.BlockSpec(memory_space=pl.ANY)
    scratch = [pltpu.VMEM((sources, BLOCK, w), bf16) for w in CHUNKS]
    scratch += [pltpu.VMEM((4, own, BLOCK, w), bf16) for w in CHUNKS]
    scratch += [pltpu.VMEM((arriving, w), bf16) for w in CHUNKS]
    scratch += [pltpu.VMEM((members * rows, w), bf16) for w in CHUNKS]
    scratch += [
        pltpu.SemaphoreType.DMA((count,)),
        pltpu.VMEM((BLOCK, BLOCK), f32),
        pltpu.VMEM((4, SLOT, 128), f32),
        pltpu.VMEM(edge_weight.shape, jnp.int32),
        pltpu.VMEM((NZ * NY * SLOT, rows), bf16),
        pltpu.VMEM((rows, nb * BLOCK), bf16),
        pltpu.VMEM((rows, BLOCK), f32),
        pltpu.VMEM((3, model, width), bf16),
        pltpu.VMEM((model, 3 * width), bf16),
        pltpu.VMEM((model, model), bf16),
        pltpu.VMEM((members * rows, 3 * width), f32),
        pltpu.VMEM((members * rows, 128), f32),
        pltpu.VMEM((rows, model), bf16),
        pltpu.VMEM((3, members * own, BLOCK, width), bf16),
        pltpu.VMEM((2 * BLOCK, keys), f32),
        pltpu.VMEM((2 * BLOCK, keys), f32),
        pltpu.VMEM((members * rows, width), bf16),
        pltpu.VMEM((members, rows, width), bf16),
        pltpu.SemaphoreType.DMA((5,)),
        pltpu.SemaphoreType.DMA,
        pltpu.SemaphoreType.DMA,
        pltpu.SemaphoreType.DMA((4,)),
        pltpu.SemaphoreType.DMA((4,)),
        pltpu.SemaphoreType.DMA((count, 4)),
        pltpu.SemaphoreType.DMA((count, 4)),
        pltpu.SemaphoreType.DMA((count,)),
        pltpu.SemaphoreType.DMA((count,)),
        pltpu.SemaphoreType.DMA((count, 4)),
        pltpu.SemaphoreType.DMA((count, 4)),
        pltpu.SemaphoreType.DMA((count, 4)),
        pltpu.SemaphoreType.DMA((count, 4)),
    ]
    return pl.pallas_call(
        layer_kernel,
        out_shape=jax.ShapeDtypeStruct((rows, model), bf16),
        in_specs=[hbm, vmem, vmem, smem, smem, vmem, hbm, hbm, hbm, hbm, hbm],
        out_specs=vmem,
        scratch_shapes=scratch,
        compiler_params=pltpu.CompilerParams(
            collective_id=1, has_side_effects=True, vmem_limit_bytes=60 * 2**20
        ),
        name="layer",
    )(
        features.reshape(own, BLOCK, model), send_rows[0], send_count, edge_blocks,
        mask_blocks[0].T, norm_gain.reshape(-1, 128), edge_weight,
        query_weight, key_weight, value_weight, out_weight,
    )


def solution(mesh):
    placed = (
        P(("graph", "attn"), None),
        P(("graph", "attn"), None, None),
        P(("graph", "attn"), None),
        P(("graph", "attn"), None),
        P(("graph", "attn"), None, None, None),
        P("graph", None, None),
        P(),
        P(),
        P(),
        P(),
        P(),
    )
    return jax.shard_map(
        on_device, mesh=mesh, in_specs=placed, out_specs=P(("graph", "attn"), None), check_vma=False
    )
```

time: 160 us -> 131 us (0.82)
  blocking collectives: 19.8 us -> 0 us
  local copies, waits for them, and re-layouts: 7.24 us -> 2.26 us
  matrix products: 2.27 us -> 0 us
    all_to_all x1 -> x0, blocking collectives: 19.8 us -> none  [on_device(): lax.all_to_all(attended, 'attn', split_axis=0, concat_axis=1, tiled=True)]
    dot_general x1 -> x0, matrix products: 2.27 us -> none  [on_device(): jnp.dot(returned, out_weight, preferred_element_type=f32)]
    reshape x1 -> x0, local copies, waits for them, and re-layouts: 1.71 us -> none  [spread(): gain.reshape(model, 1)]
    unnamed x8 -> x1, local copies, waits for them, and re-layouts: 3.61 us -> 2.26 us
    pallas_call x2 -> x1, Pallas kernels: 130 us -> 129 us  [on_device(): pl.pallas_call(layer_kernel, out_shape=jax.ShapeDtypeStruct((rows, model)...]
where the time goes in v3:
time: 131 us
  Pallas kernels  129 us (98%)
  local copies, waits for them, and re-layouts  2.26 us (2%)
    pallas_call x1, Pallas kernels, on_device(): pl.pallas_call(layer_kernel, out_shape=jax.ShapeDtypeStruct((rows, model)...  129 us

profile of v3, /device:TPU:1, one launch (start us, length us, event | category | flops | bytes accessed | tf_op | source)
XLA Modules:
  0.0 130.8 jit_solution(7661925241479189872)
XLA Ops:
  0.0 128.6 %layer.1 = bf16[512,1024]{1,0:T(8,128)(2,1)} custom-call(bf16[4,128,1024]{2,1,0:T(8,128)(2,1)} %bitcast.6, s32[32,64]{1,0:T(8,128)} %bitcast.7, s32[1,32]{1,0:T(1,128)} %send_count.1, s32[4,6]{1,0:T(4,128)} %blocks_ref.1, s32[16,32]{1,0:T(8,128)} %bitcast.8, f32[8,128]{1,0:T(8,128)} %bitcast.9, s32[4,6,128,128]{3,2,1,0:T(8,128)} %edges_hbm.1, ...), custom_call_target="tpu_custom_call" | custom-call | tf_op jit(solution)/shard_map/layer/pallas_call | solution.py:477
  128.6 2.3 %copy.13 = bf16[512,1024]{1,0:T(8,128)(2,1)} copy(bf16[512,1024]{1,0:T(8,128)(2,1)} %layer.1) | data formatting | bytes 2097152

commit v4 on v3

--- a/solution.py
+++ b/solution.py
@@ -13,7 +13,7 @@
 NY = 4
 NX = 4
 SLOT = 64
-CHUNKS = (256, 256, 256, 256)
+CHUNKS = (512, 256, 256)
 AHEAD = 1
 PLUS = (0, 1)
 MINUS = (2, 3)
@@ -23,7 +23,7 @@
 
 def layer_kernel(
     features, send_rows, send_count, blocks_ref, mask_ref, gain, edges_hbm,
-    query_hbm, key_hbm, value_hbm, out_hbm, result, *scratch,
+    query_hbm, key_hbm, value_hbm, mixed_hbm, own_hbm, *scratch,
 ):
     count = len(CHUNKS)
     starts = [sum(CHUNKS[:c]) for c in range(count)]
@@ -33,7 +33,7 @@
     staged = [scratch.pop(0) for _ in range(count)]
     gathered = [scratch.pop(0) for _ in range(count)]
     (
-        feature_sem, slots, slots_in, edges, picks, weights, scale, columns, folded, out_weight, total, squares,
+        feature_sem, slots, slots_in, edges, picks, weights, scale, columns, folded, total, squares,
         own_out, joined, scores_a, scores_b, mixed_out, mixed_in,
         column_sem, mixed_send, mixed_recv, slot_send, slot_recv, table_send, table_recv, halo_send, halo_recv,
         ring_send, ring_recv, pair_send, pair_recv,
@@ -66,7 +66,6 @@
         for k, ref in enumerate((query_hbm, key_hbm, value_hbm))
     ]
     loads.append(pltpu.make_async_copy(edges_hbm, edges, column_sem.at[3]))
-    loads.append(pltpu.make_async_copy(out_hbm, out_weight, column_sem.at[4]))
     feature_loads = [
         pltpu.make_async_copy(
             features.at[:, :, pl.ds(starts[c], CHUNKS[c])], source[c].at[0:own], feature_sem.at[c]
@@ -127,16 +126,13 @@
     for side in (1, -1):
         plan.append((-side, [(0, dy) for dy in range(NY)]))
     for side, far in ((1, PLUS), (-1, MINUS)):
-        plan.append(
-            (
-                -2 * side,
-                [(0, dy) for dy in range(NY)]
-                + [(side, dy) for dy in range(NY)]
-                + [(2 * side, dy) for dy in far],
-            )
-        )
+        onward = [(side, dy) for dy in range(NY)] + [(2 * side, dy) for dy in far]
+        plan.append((-2 * side, onward))
+    for side in (1, -1):
+        plan.append((-2 * side, [(0, dy) for dy in range(NY)]))
+    keeps = [int(p[1][0] == (0, 0)) for p in plan]
     pick_start = [sum(len(p[1]) for p in plan[:k]) * SLOT for k in range(len(plan))]
-    stage_start = [sum(len(p[1]) - 1 for p in plan[:k]) * SLOT for k in range(len(plan))]
+    stage_start = [pick_start[k] - sum(keeps[:k]) * SLOT for k in range(len(plan))]
 
     lane = lax.broadcasted_iota(jnp.int32, (SLOT, 128), 1)
     row_number = lax.broadcasted_iota(jnp.int32, (SLOT, rows), 1).astype(f32)
@@ -162,10 +158,12 @@
         found = jnp.dot(
             picks[pick_start[k] : pick_start[k] + size, :], table, preferred_element_type=f32
         ).astype(bf16)
-        source[c][(*halo_rows(sender), slice(None))] = found[0:SLOT]
+        kept = keeps[k]
+        if kept:
+            source[c][(*halo_rows(sender), slice(None))] = found[0:SLOT]
         at = stage_start[k]
-        staged[c][at : at + size - SLOT, :] = found[SLOT:]
-        for n, (dz, dy) in enumerate(dests[1:]):
+        staged[c][at : at + size - kept * SLOT, :] = found[kept * SLOT :]
+        for n, (dz, dy) in enumerate(dests[kept:]):
             go(
                 remote(
                     staged[c].at[at + n * SLOT : at + (n + 1) * SLOT],
@@ -175,15 +173,18 @@
             )
 
     def first_hop(c):
-        extract(c, 0, source[c][0:own].reshape(rows, CHUNKS[c]))
+        if c == 0:
+            extract(c, 0, source[c][0:own].reshape(rows, CHUNKS[c]))
         for k in range(2):
             if c == 0:
                 slot_copy(k, slots.at[0:SLOT]).wait_recv()
                 go(slot_copy(k + 2, slots_in.at[k]))
             table_copy(c, k, source[c].at[0:own]).wait_recv()
             go(table_copy(c, k + 2, tables[c].at[k]))
-        if c + AHEAD < count:
-            send_own(c + AHEAD)
+        if AHEAD == 1 and c + 1 < count:
+            send_own(c + 1)
+        if c > 0:
+            extract(c, 0, source[c][0:own].reshape(rows, CHUNKS[c]))
         for k in range(2):
             if c == 0:
                 build(k + 1, slots_in.at[k])
@@ -194,15 +195,21 @@
             if c == 0:
                 slot_copy(k, slots.at[0:SLOT]).wait_recv()
                 build(k + 1, slots_in.at[k])
+                build(k + 3, slots_in.at[k])
             table_copy(c, k, source[c].at[0:own]).wait_recv()
             extract(c, k + 1, tables[c][k].reshape(rows, CHUNKS[c]))
+        if AHEAD == 2 and c + 2 < count:
+            send_own(c + 2)
+        for k in range(2, 4):
+            extract(c, k + 3, tables[c][k].reshape(rows, CHUNKS[c]))
 
     def slot_rows(owner, low=0, high=None):
         high = rows if high is None else high
         return pl.ds(pl.multiple_of(owner * rows + low, BLOCK), high - low)
 
     half = rows // 2
-    pieces = [(0, 0, rows), (0, 0, rows), (-1, 0, half), (1, half, rows)]
+    pieces = [(0, 0, half), (0, half, rows), (0, half, rows), (0, 0, half)]
+    pieces += [(-1, 0, half), (1, half, rows)]
 
     def ring_copy(c, k):
         dx, low, high = pieces[k]
@@ -230,50 +237,61 @@
             gathered[c][
                 pl.ds(pl.multiple_of(attn * rows + b * BLOCK, BLOCK), BLOCK), :
             ] = mixed
-        go(ring_copy(c, 0))
+            if (b + 1) * BLOCK == half:
+                go(ring_copy(c, 0))
         go(ring_copy(c, 1))
+        go(ring_copy(c, 2))
+        go(ring_copy(c, 3))
         go(pair_copy(c, 0))
 
     def pass_on(c):
         for k in range(2):
             ring_copy(c, k).wait_recv()
-            go(ring_copy(c, k + 2))
+            go(ring_copy(c, k + 4))
+        for k in range(2):
+            ring_copy(c, k + 2).wait_recv()
             go(pair_copy(c, k + 1))
 
     def pass_last(c):
-        for k in range(2, 4):
+        for k in range(4, 6):
             ring_copy(c, k).wait_recv()
         go(pair_copy(c, 3))
 
-    def project(c):
+    last = count - 1
+
+    def squared_sum(values):
+        wide = values.astype(f32)
+        wide = wide * wide
+        return sum(wide[:, i : i + 128] for i in range(0, values.shape[1], 128))
+
+    def project_first(low, high):
+        def one(owner, carry):
+            at = slot_rows(owner)
+            parts = [gathered[c][at, :] for c in range(last)]
+            total[at, :] = jnp.dot(
+                jnp.concatenate(parts, axis=1), folded[0 : starts[last], :],
+                preferred_element_type=f32,
+            )
+            squares[at, :] = sum(squared_sum(values) for values in parts)
+            return carry
+
+        lax.fori_loop(low, high, one, 0)
+
+    def project_last(owner):
+        at = slot_rows(owner)
+        values = gathered[last][at, :]
+        made = total[at, :] + jnp.dot(values, folded[starts[last] :, :], preferred_element_type=f32)
+        squared = squares[at, :] + squared_sum(values)
+        mean = jnp.sum(squared, axis=1, keepdims=True) * (1.0 / sum(CHUNKS))
+        made = (made * lax.rsqrt(mean + EPSILON)).astype(bf16)
+        for k in range(3):
+            joined[k, pl.ds(owner * own, own)] = made[:, k * width : (k + 1) * width].reshape(
+                own, BLOCK, width
+            )
+
+    def pair_wait(c):
         for k in range(4):
             pair_copy(c, k).wait_recv()
-
-        def one(owner, carry):
-            at = slot_rows(owner)
-            values = gathered[c][at, :]
-            made = jnp.dot(
-                values, folded[starts[c] : starts[c] + CHUNKS[c], :], preferred_element_type=f32
-            )
-            wide = values.astype(f32)
-            wide = wide * wide
-            squared = sum(wide[:, i : i + 128] for i in range(0, CHUNKS[c], 128))
-            if c > 0:
-                made = made + total[at, :]
-                squared = squared + squares[at, :]
-            if c + 1 < count:
-                total[at, :] = made
-                squares[at, :] = squared
-            else:
-                mean = jnp.sum(squared, axis=1, keepdims=True) * (1.0 / sum(CHUNKS))
-                made = (made * lax.rsqrt(mean + EPSILON)).astype(bf16)
-                for k in range(3):
-                    joined[k, pl.ds(owner * own, own)] = made[
-                        :, k * width : (k + 1) * width
-                    ].reshape(own, BLOCK, width)
-            return carry
-
-        lax.fori_loop(0, 2 * NX, one, 0)
 
     build(0, slots.at[0:SLOT])
     for c in range(count):
@@ -303,19 +321,29 @@
             pass_last(c - 2)
         if c >= 1:
             blend(c - 1)
-        if c >= 2:
-            project(c - 2)
         second_hop(c)
         if c >= 1:
             pass_on(c - 1)
-    if count >= 2:
-        pass_last(count - 2)
-    blend(count - 1)
-    if count >= 2:
-        project(count - 2)
-    pass_on(count - 1)
-    pass_last(count - 1)
-    project(count - 1)
+    blend(last)
+    pass_last(last - 1)
+    for c in range(last):
+        pair_wait(c)
+    own_store = pltpu.make_async_copy(own_out, own_hbm, feature_sem.at[0])
+    own_store.start()
+    project_first(0, NX)
+    pass_on(last)
+    project_first(NX, 2 * NX)
+
+    def near_member(index, carry):
+        project_last(peer(index + index // 2))
+        return carry
+
+    lax.fori_loop(0, 3, near_member, 0)
+    pass_last(last)
+    project_last(peer(2))
+    for k in range(4):
+        pair_copy(last, k).wait_recv()
+        project_last(peer((0, -1, 1, 2)[k], 1))
 
     first = lax.broadcasted_iota(jnp.int32, (BLOCK, width), 1) < HEAD_DIM
     ones = jnp.ones((2 * BLOCK, width), bf16)
@@ -352,60 +380,50 @@
         sums = sums[:, :width] / sums[:, width:]
         return jnp.where(first, sums[:BLOCK], sums[BLOCK:]).astype(bf16)
 
-    def mixed_copy(owner, low):
-        return remote(
-            mixed_out.at[pl.ds(pl.multiple_of(owner * rows + low, BLOCK), 2 * BLOCK)],
-            mixed_in.at[attn, pl.ds(pl.multiple_of(low, BLOCK), 2 * BLOCK)],
-            mixed_send, mixed_recv, (graph, owner),
-        )
-
-    def attend(index):
-        owner = lax.rem(attn + 1 + index // 2, 2 * NX)
-        low = lax.rem(index, 2) * (2 * BLOCK)
-        block = owner * own + lax.rem(index, 2) * 2
-        top_a = score(block, scores_a)
-        top_b = score(block + 1, scores_b)
-        low_rows = mix(block, scores_a, top_a)
-        high_rows = mix(block + 1, scores_b, top_b)
-        return owner, low, low_rows, high_rows
-
-    def away(index, carry):
-        owner, low, low_rows, high_rows = attend(index)
-        at = pl.multiple_of(owner * rows + low, BLOCK)
-        mixed_out[pl.ds(at, BLOCK), :] = low_rows
-        mixed_out[pl.ds(pl.multiple_of(at + BLOCK, BLOCK), BLOCK), :] = high_rows
-        mixed_copy(owner, low).start()
+    def attend(index, carry):
+        owner = lax.rem(attn + 1 + index, 2 * NX)
+        block = owner * own
+        made = []
+        for low in range(0, own, 2):
+            top_a = score(block + low, scores_a)
+            top_b = score(block + low + 1, scores_b)
+            made.append(mix(block + low, scores_a, top_a))
+            made.append(mix(block + low + 1, scores_b, top_b))
+        at = pl.ds(pl.multiple_of(owner * rows, rows), rows)
+        mixed_out[at, :] = jnp.concatenate(made, axis=0)
+
+        @pl.when(index < 2 * NX - 1)
+        def _():
+            remote(
+                mixed_out.at[at], mixed_in.at[:, pl.ds(first_col, width)],
+                mixed_send, mixed_recv, (graph, owner),
+            ).start()
+
+        @pl.when(index == 2 * NX - 1)
+        def _():
+            mixed_in[:, pl.ds(first_col, width)] = mixed_out[at, :]
+
         return carry
 
-    def home(index, carry):
-        owner, low, low_rows, high_rows = attend(index)
-        at = pl.multiple_of(low, BLOCK)
-        mixed_in[attn, pl.ds(at, BLOCK), :] = low_rows
-        mixed_in[attn, pl.ds(pl.multiple_of(at + BLOCK, BLOCK), BLOCK), :] = high_rows
-        return carry
-
-    lax.fori_loop(0, 4 * NX - 2, away, 0)
-    lax.fori_loop(4 * NX - 2, 4 * NX, home, 0)
+    lax.fori_loop(0, 2 * NX, attend, 0)
     returned = remote(
         mixed_out.at[0 : (2 * NX - 1) * rows], mixed_out.at[0 : (2 * NX - 1) * rows],
         mixed_send, mixed_recv, (graph, peer(0, 1)),
     )
-    loads[4].wait()
     returned.wait_recv()
-    for b in range(own):
-        here = slice(b * BLOCK, (b + 1) * BLOCK)
-        attended = jnp.concatenate([mixed_in[k, here, :] for k in range(2 * NX)], axis=1)
-        made = jnp.dot(attended, out_weight[...], preferred_element_type=f32)
-        result[here, :] = (made + own_out[here, :].astype(f32)).astype(bf16)
-
+    mixed_store = pltpu.make_async_copy(mixed_in, mixed_hbm, feature_sem.at[1])
+    mixed_store.start()
     returned.wait_send()
+    own_store.wait()
+    mixed_store.wait()
     for k in range(4):
         slot_copy(k, slots.at[0:SLOT]).wait_send()
     for c in range(count):
         for k in range(4):
             table_copy(c, k, source[c].at[0:own]).wait_send()
+            pair_copy(c, k).wait_send()
+        for k in range(6):
             ring_copy(c, k).wait_send()
-            pair_copy(c, k).wait_send()
         remote(
             staged[c], staged[c],
             halo_send.at[c], halo_recv.at[c], (graph, peer(0, 1)),
@@ -451,7 +469,6 @@
         pltpu.VMEM((rows, BLOCK), f32),
         pltpu.VMEM((3, model, width), bf16),
         pltpu.VMEM((model, 3 * width), bf16),
-        pltpu.VMEM((model, model), bf16),
         pltpu.VMEM((members * rows, 3 * width), f32),
         pltpu.VMEM((members * rows, 128), f32),
         pltpu.VMEM((rows, model), bf16),
@@ -459,8 +476,8 @@
         pltpu.VMEM((2 * BLOCK, keys), f32),
         pltpu.VMEM((2 * BLOCK, keys), f32),
         pltpu.VMEM((members * rows, width), bf16),
-        pltpu.VMEM((members, rows, width), bf16),
-        pltpu.SemaphoreType.DMA((5,)),
+        pltpu.VMEM((rows, model), bf16),
+        pltpu.SemaphoreType.DMA((4,)),
         pltpu.SemaphoreType.DMA,
         pltpu.SemaphoreType.DMA,
         pltpu.SemaphoreType.DMA((4,)),
@@ -469,16 +486,16 @@
         pltpu.SemaphoreType.DMA((count, 4)),
         pltpu.SemaphoreType.DMA((count,)),
         pltpu.SemaphoreType.DMA((count,)),
-        pltpu.SemaphoreType.DMA((count, 4)),
-        pltpu.SemaphoreType.DMA((count, 4)),
+        pltpu.SemaphoreType.DMA((count, 6)),
+        pltpu.SemaphoreType.DMA((count, 6)),
         pltpu.SemaphoreType.DMA((count, 4)),
         pltpu.SemaphoreType.DMA((count, 4)),
     ]
-    return pl.pallas_call(
+    attended, aggregated = pl.pallas_call(
         layer_kernel,
-        out_shape=jax.ShapeDtypeStruct((rows, model), bf16),
-        in_specs=[hbm, vmem, vmem, smem, smem, vmem, hbm, hbm, hbm, hbm, hbm],
-        out_specs=vmem,
+        out_shape=(jax.ShapeDtypeStruct((rows, model), bf16),) * 2,
+        in_specs=[hbm, vmem, vmem, smem, smem, vmem, hbm, hbm, hbm, hbm],
+        out_specs=(hbm, hbm),
         scratch_shapes=scratch,
         compiler_params=pltpu.CompilerParams(
             collective_id=1, has_side_effects=True, vmem_limit_bytes=60 * 2**20
@@ -487,8 +504,10 @@
     )(
         features.reshape(own, BLOCK, model), send_rows[0], send_count, edge_blocks,
         mask_blocks[0].T, norm_gain.reshape(-1, 128), edge_weight,
-        query_weight, key_weight, value_weight, out_weight,
+        query_weight, key_weight, value_weight,
     )
+    updated = jnp.dot(attended, out_weight, preferred_element_type=f32)
+    return (updated + aggregated.astype(f32)).astype(bf16)
 
 
 def solution(mesh):

time: 131 us -> 127 us (0.969)
  Pallas kernels: 129 us -> 122 us
  matrix products: 0 us -> 3.77 us
  local copies, waits for them, and re-layouts: 2.26 us -> 0.01 us
    pallas_call x1, Pallas kernels: 129 us -> 122 us  [on_device(): pl.pallas_call(layer_kernel, out_shape=(jax.ShapeDtypeStruct((rows, model...]
    dot_general x0 -> x1, matrix products: none -> 3.77 us  [on_device(): updated = jnp.dot(attended, out_weight, preferred_element_type=f32)]
    unnamed x1 -> x2, local copies, waits for them, and re-layouts: 2.26 us -> 0.01 us
where the time goes in v4:
time: 127 us; the launch traced here: 126 us
  Pallas kernels  122 us (96%)
  matrix products  3.77 us (3%)
    pallas_call x1, Pallas kernels, on_device(): pl.pallas_call(layer_kernel, out_shape=(jax.ShapeDtypeStruct((rows, model...  122 us
    dot_general x1, matrix products, on_device(): updated = jnp.dot(attended, out_weight, preferred_element_type=f32)  3.77 us

profile of v4, /device:TPU:1, one launch (start us, length us, event | category | flops | bytes accessed | tf_op | source)
XLA Modules:
  0.0 126.0 jit_solution(17120707179594803342)
XLA Ops:
  0.0 0.0 copy-start
  0.0 122.2 %layer.1 = (bf16[512,1024]{1,0:T(8,128)(2,1)}, bf16[512,1024]{1,0:T(8,128)(2,1)}) custom-call(bf16[4,128,1024]{2,1,0:T(8,128)(2,1)} %bitcast.8, s32[32,64]{1,0:T(8,128)} %bitcast.9, s32[1,32]{1,0:T(1,128)} %send_count.1, s32[4,6]{1,0:T(4,128)} %blocks_ref.1, s32[16,32]{1,0:T(8,128)} %bitcast.10, f32[8,128]{1,0:T(8,128)} %bitcast.11, ...), custom_call_target="tpu_custom_call" | custom-call | tf_op jit(solution)/shard_map/layer/pallas_call | solution.py:494
  122.2 0.0 copy-done
  122.2 3.8 %add_convert_fusion = bf16[512,1024]{1,0:T(8,128)(2,1)} fusion(bf16[512,1024]{1,0:T(8,128)(2,1)} %get-tuple-element.8, bf16[512,1024]{1,0:T(8,128)(2,1)} %get-tuple-element.7, bf16[1024,1024]{1,0:T(8,128)(2,1)S(1)} %copy-done), kind=kOutput, calls=%fused_computation | convolution fusion | flops 1075314688 | bytes 5242880 | tf_op jit(solution)/shard_map/dot_general | solution.py:509
Async XLA Ops:
  0.0 122.2 %copy-start = (bf16[1024,1024]{1,0:T(8,128)(2,1)S(1)}, bf16[1024,1024]{1,0:T(8,128)(2,1)}, u32[]{:S(2)}) copy-start(bf16[1024,1024]{1,0:T(8,128)(2,1)} %param.21) | copy-start | bytes 6291460

commit v5 on v4

--- a/solution.py
+++ b/solution.py
@@ -264,15 +264,19 @@
         wide = wide * wide
         return sum(wide[:, i : i + 128] for i in range(0, values.shape[1], 128))
 
-    def project_first(low, high):
+    def project_early(c, low, high):
         def one(owner, carry):
             at = slot_rows(owner)
-            parts = [gathered[c][at, :] for c in range(last)]
-            total[at, :] = jnp.dot(
-                jnp.concatenate(parts, axis=1), folded[0 : starts[last], :],
-                preferred_element_type=f32,
+            values = gathered[c][at, :]
+            made = jnp.dot(
+                values, folded[starts[c] : starts[c] + CHUNKS[c], :], preferred_element_type=f32
             )
-            squares[at, :] = sum(squared_sum(values) for values in parts)
+            squared = squared_sum(values)
+            if c > 0:
+                made = made + total[at, :]
+                squared = squared + squares[at, :]
+            total[at, :] = made
+            squares[at, :] = squared
             return carry
 
         lax.fori_loop(low, high, one, 0)
@@ -324,15 +328,17 @@
         second_hop(c)
         if c >= 1:
             pass_on(c - 1)
+        if c >= 2:
+            pair_wait(c - 2)
+            project_early(c - 2, 0, 2 * NX)
     blend(last)
     pass_last(last - 1)
-    for c in range(last):
-        pair_wait(c)
+    pair_wait(last - 1)
     own_store = pltpu.make_async_copy(own_out, own_hbm, feature_sem.at[0])
     own_store.start()
-    project_first(0, NX)
+    project_early(last - 1, 0, NX)
     pass_on(last)
-    project_first(NX, 2 * NX)
+    project_early(last - 1, NX, 2 * NX)
 
     def near_member(index, carry):
         project_last(peer(index + index // 2))

time: 127 us -> 127 us (level)
  no operation moved by 1% of the time
where the time goes in v5:
time: 127 us; the launch traced here: 126 us
  Pallas kernels  122 us (96%)
  matrix products  3.77 us (3%)
    pallas_call x1, Pallas kernels, on_device(): pl.pallas_call(layer_kernel, out_shape=(jax.ShapeDtypeStruct((rows, model...  122 us
    dot_general x1, matrix products, on_device(): updated = jnp.dot(attended, out_weight, preferred_element_type=f32)  3.77 us

profile of v5, /device:TPU:1, one launch (start us, length us, event | category | flops | bytes accessed | tf_op | source)
XLA Modules:
  0.0 125.9 jit_solution(5830608676952143662)
XLA Ops:
  0.0 0.0 copy-start
  0.0 122.1 %layer.1 = (bf16[512,1024]{1,0:T(8,128)(2,1)}, bf16[512,1024]{1,0:T(8,128)(2,1)}) custom-call(bf16[4,128,1024]{2,1,0:T(8,128)(2,1)} %bitcast.8, s32[32,64]{1,0:T(8,128)} %bitcast.9, s32[1,32]{1,0:T(1,128)} %send_count.1, s32[4,6]{1,0:T(4,128)} %blocks_ref.1, s32[16,32]{1,0:T(8,128)} %bitcast.10, f32[8,128]{1,0:T(8,128)} %bitcast.11, ...), custom_call_target="tpu_custom_call" | custom-call | tf_op jit(solution)/shard_map/layer/pallas_call | solution.py:500
  122.1 0.0 copy-done
  122.1 3.8 %add_convert_fusion = bf16[512,1024]{1,0:T(8,128)(2,1)} fusion(bf16[512,1024]{1,0:T(8,128)(2,1)} %get-tuple-element.8, bf16[512,1024]{1,0:T(8,128)(2,1)} %get-tuple-element.7, bf16[1024,1024]{1,0:T(8,128)(2,1)S(1)} %copy-done), kind=kOutput, calls=%fused_computation | convolution fusion | flops 1075314688 | bytes 5242880 | tf_op jit(solution)/shard_map/dot_general | solution.py:515
Async XLA Ops:
  0.0 122.1 %copy-start = (bf16[1024,1024]{1,0:T(8,128)(2,1)S(1)}, bf16[1024,1024]{1,0:T(8,128)(2,1)}, u32[]{:S(2)}) copy-start(bf16[1024,1024]{1,0:T(8,128)(2,1)} %param.21) | copy-start | bytes 6291460
